TPU v7x, 512 devices: a whole 4x8x8 slice. The times are simulated.
512 devices in a mesh: rep: 16 (over x, y_lo), fsdp: 32 (over z, y_hi, core).
Axes of the slice: x: 4, y: 8 (y_hi: 2, y_lo: 4; y = y_hi * 4 + y_lo), z: 8, core: 2. Of those that a mesh axis runs over, the one named last changes fastest.
Arguments:
- tokens: bfloat16 [122880, 4096], P(('rep', 'fsdp')), may hold values from -24 to 24
- norm_gain: bfloat16 [4096], replicated, may hold values from 0.5 to 1.5
- weight: bfloat16 [16, 4096, 512], P('rep', 'fsdp'), may hold values from -6 to 6
- momentum: bfloat16 [16, 4096, 512], P('rep', 'fsdp'), may hold values from -4 to 4
- key_grad: bfloat16 [122880, 512], P(('rep', 'fsdp')), may hold values from -4.1875 to 4.1875
- matching: int32 [16], replicated, may hold values from 0 to 15, as said below
Outputs:
- keys: bfloat16 [122880, 512], P(('rep', 'fsdp'))
- token_grad: bfloat16 [122880, 4096], P(('rep', 'fsdp'))
- new_weight: bfloat16 [16, 4096, 512], P('rep', 'fsdp')
- new_momentum: bfloat16 [16, 4096, 512], P('rep', 'fsdp')
Inputs may be any that keep to these rules, and one draw needn't show every extreme that they name: matching is a permutation of the 16 groups.
All inputs are finite; a program needn't handle non-finite values.
Results may differ from a plain program's by a relative error of at most 0.02.
Values may be sent and summed in bfloat16 or wider, within the bound.
No kernel may reach another device: no remote copies, remote signals or barrier semaphores. Data moves between devices by JAX's collectives and lax.ppermute only.
A program may use at most 64 MiB of HBM per device.

v0:
```python
import jax
import jax.numpy as jnp
from jax import lax
from jax.sharding import PartitionSpec as P

epsilon = 1e-05
momentum_decay = 0.9
outer_rate = 0.7


def nesterov(mean_weight, mean_momentum, grad_f):
    momentum_next = momentum_decay * mean_momentum + grad_f
    new_weight = (mean_weight - outer_rate * (grad_f + momentum_decay * momentum_next)).astype(
        jnp.bfloat16
    )
    return (new_weight, momentum_next.astype(jnp.bfloat16))


def per_device(tokens, norm_gain, weight, momentum, key_grad, matching):
    width = tokens.shape[1]
    width_scale = float(width) ** (-0.5)
    tokens_f = tokens.astype(jnp.float32)
    gain_f = norm_gain.astype(jnp.float32)
    inverse_rms = lax.rsqrt(jnp.mean(tokens_f * tokens_f, axis=-1, keepdims=True) + epsilon)
    normed = (tokens_f * inverse_rms * gain_f).astype(jnp.bfloat16)
    local_weight = weight[0]
    columns = normed
    keys_f = jnp.dot(
        columns,
        lax.all_gather(local_weight, "fsdp", axis=0, tiled=True),
        preferred_element_type=jnp.float32,
    )
    normed_grad_f = lax.dot_general(
        key_grad,
        lax.all_gather(local_weight, "fsdp", axis=0, tiled=True),
        (((1,), (1,)), ((), ())),
        preferred_element_type=jnp.float32,
    )
    keys = (keys_f * width_scale).astype(jnp.bfloat16)
    normed_grad = (normed_grad_f * width_scale).astype(jnp.bfloat16)
    upstream = normed_grad.astype(jnp.float32) * gain_f
    mixed = jnp.mean(upstream * tokens_f, axis=-1, keepdims=True)
    token_grad = (inverse_rms * (upstream - tokens_f * inverse_rms * inverse_rms * mixed)).astype(
        jnp.bfloat16
    )
    columns = normed
    grad = lax.psum_scatter(
        (
            lax.dot_general(
                columns, key_grad, (((0,), (0,)), ((), ())), preferred_element_type=jnp.float32
            )
            * width_scale
        ).astype(jnp.bfloat16),
        "fsdp",
        scatter_dimension=0,
        tiled=True,
    )
    partner = jnp.sum(
        jnp.where(jnp.arange(matching.shape[0]) == lax.axis_index("rep"), matching, 0)
    )
    pieces = (
        lax.all_gather(weight, "rep", axis=0, tiled=True),
        lax.all_gather(momentum, "rep", axis=0, tiled=True),
    )
    count = pieces[0].shape[0]
    chosen = (jnp.arange(count) == partner).astype(jnp.float32)[:, None, None]
    other_weight = jnp.sum(pieces[0].astype(jnp.float32) * chosen, axis=0)
    other_momentum = jnp.sum(pieces[1].astype(jnp.float32) * chosen, axis=0)
    mean_weight = (local_weight.astype(jnp.float32) + other_weight) * 0.5
    mean_momentum = (momentum[0].astype(jnp.float32) + other_momentum) * 0.5
    updated_weight, updated_momentum = nesterov(
        mean_weight, mean_momentum, grad.astype(jnp.float32)
    )
    new_weight = updated_weight[None]
    new_momentum = updated_momentum[None]
    return (keys, token_grad, new_weight, new_momentum)


def solution(mesh):
    in_specs = (
        P(("rep", "fsdp"), None),
        P(),
        P("rep", "fsdp", None),
        P("rep", "fsdp", None),
        P(("rep", "fsdp"), None),
        P(),
    )
    out_specs = (
        P(("rep", "fsdp"), None),
        P(("rep", "fsdp"), None),
        P("rep", "fsdp", None),
        P("rep", "fsdp", None),
    )
    return jax.shard_map(
        per_device, mesh=mesh, in_specs=in_specs, out_specs=out_specs, check_vma=False
    )
```

profile of v0, /device:TPU:1, one launch (start us, length us, event | category | flops | bytes accessed | tf_op | source)
XLA Modules:
  0.0 458.5 jit_solution(2044992985265275165)
XLA Ops:
  7.2 0.0 copy-start
  7.2 0.0 all-gather.9.cloned.1.call-start
  7.2 0.7 all-gather.9.cloned.1.call-update
  7.9 0.0 all-gather.7.cloned.1.call-start
  8.0 0.7 all-gather.7.cloned.1.call-update
  8.7 0.0 all-gather.5.cloned.1.call-start
  8.7 0.7 all-gather.5.cloned.1.call-update
  9.4 0.0 reduce-scatter.2.cloned.1.call-start
  9.4 0.7 convert_element_type.56
  10.1 0.0 copy-start.2
  10.1 114.8 %all-gather.9.cloned.1.call-done = bf16[1,4096,512]{2,1,0:T(8,128)(2,1)} async-done(((bf16[1,128,512]{2,1,0:T(8,128)(2,1)}), bf16[1,4096,512]{2,1,0:T(8,128)(2,1)}) %all-gather.9.cloned.1.call-update) | async-done | bytes 4194320 | tf_op jit(solution)/shard_map/all_gather | solution.py:30
  125.0 0.0 copy-done
  125.0 6.1 %fusion.14 = (f32[240]{0:T(256)S(1)}, f32[240]{0:T(256)S(1)}, f32[240,4096]{1,0:T(8,128)}) fusion(bf16[240,4096]{1,0:T(8,128)(2,1)} %param.6, f32[4096]{0:T(1024)S(1)} %convert_element_type.56, bf16[240,512]{1,0:T(8,128)(2,1)S(1)} %copy-done, bf16[1,4096,512]{2,1,0:T(8,128)(2,1)} %all-gather.9.cloned.1.call-done), kind=kOutput, calls=%fused_computation.21 | convolution fusion | flops 1015479808 | bytes 10356608 | tf_op jit(solution)/shard_map/dot_general | solution.py:33
  131.1 0.0 copy-done.2
  131.1 3.4 multiply_convert_fusion
  134.5 0.0 copy-start.6
  134.6 0.0 reduce-scatter.2.cloned.1.call-update
  134.6 0.6 copy-done.6
  135.2 0.6 fusion.31
  135.8 0.6 compare_convert_fusion
  136.5 63.6 %all-gather.7.cloned.1.call-done = bf16[16,128,512]{2,1,0:T(8,128)(2,1)} async-done(((bf16[1,128,512]{2,1,0:T(8,128)(2,1)}), bf16[16,128,512]{2,1,0:T(8,128)(2,1)}) %all-gather.7.cloned.1.call-update) | async-done | bytes 2097168 | tf_op jit(solution)/shard_map/all_gather | solution.py:63
  200.1 91.7 %all-gather.5.cloned.1.call-done = bf16[16,128,512]{2,1,0:T(8,128)(2,1)} async-done(((bf16[1,128,512]{2,1,0:T(8,128)(2,1)}), bf16[16,128,512]{2,1,0:T(8,128)(2,1)}) %all-gather.5.cloned.1.call-update) | async-done | bytes 2097168 | tf_op jit(solution)/shard_map/all_gather | solution.py:62
  291.8 0.0 copy-start.5
  291.8 3.3 multiply_reduce_fusion
  295.2 0.1 copy-done.5
  295.3 0.0 copy-start.1
  295.3 1.9 fusion.18
  297.2 0.2 copy-done.1
  297.4 0.0 copy-start.3
  297.4 0.0 copy-start.4
  297.4 2.4 fusion.12
  299.8 150.5 %reduce-scatter.2.cloned.1.call-done = bf16[128,512]{1,0:T(8,128)(2,1)} async-done(((bf16[4096,512]{1,0:T(8,128)(2,1)}), bf16[128,512]{1,0:T(8,128)(2,1)}) %reduce-scatter.2.cloned.1.call-update) | async-done | bytes 131088 | tf_op jit(solution)/shard_map/reduce_scatter | solution.py:47
  450.3 0.0 copy-done.3
  450.3 0.0 copy-done.4
  450.3 1.7 fusion.30
  (2 shorter events, 0.0 us)
Async XLA Ops:
  7.2 117.8 %copy-start = (bf16[240,512]{1,0:T(8,128)(2,1)S(1)}, bf16[240,512]{1,0:T(8,128)(2,1)}, u32[]{:S(2)}) copy-start(bf16[240,512]{1,0:T(8,128)(2,1)} %param.10) | copy-start | bytes 737284
  7.2 117.8 %all-gather.9.cloned.1.call-start = ((), (), s32[]{:S(2)}) async-start(), calls=%async_computation.4 | async-start | bytes 4325376 | tf_op jit(solution)/shard_map/all_gather | solution.py:30
  7.9 192.2 %all-gather.7.cloned.1.call-start = ((), (), s32[]{:S(2)}) async-start(), calls=%async_computation.3 | async-start | bytes 2228224 | tf_op jit(solution)/shard_map/all_gather | solution.py:63
  8.7 283.1 %all-gather.5.cloned.1.call-start = ((), (), s32[]{:S(2)}) async-start(), calls=%async_computation.1 | async-start | bytes 2228224 | tf_op jit(solution)/shard_map/all_gather | solution.py:62
  9.4 440.9 %reduce-scatter.2.cloned.1.call-start = ((), (), s32[]{:S(2)}) async-start(), calls=%async_computation.2 | async-start | bytes 4325376 | tf_op jit(solution)/shard_map/reduce_scatter | solution.py:47
  10.1 121.0 %copy-start.2 = (bf16[240,4096]{1,0:T(8,128)(2,1)S(1)}, bf16[240,4096]{1,0:T(8,128)(2,1)}, u32[]{:S(2)}) copy-start(bf16[240,4096]{1,0:T(8,128)(2,1)} %param.6) | copy-start | bytes 5898244
  134.5 0.7 copy-start.6
  291.8 3.4 copy-start.5
  295.3 2.1 copy-start.1
  297.4 152.9 %copy-start.3 = (bf16[1,128,512]{2,1,0:T(8,128)(2,1)S(1)}, bf16[1,128,512]{2,1,0:T(8,128)(2,1)}, u32[]{:S(2)}) copy-start(bf16[1,128,512]{2,1,0:T(8,128)(2,1)} %param.8) | copy-start | bytes 393220
  297.4 152.9 %copy-start.4 = (bf16[1,128,512]{2,1,0:T(8,128)(2,1)S(1)}, bf16[1,128,512]{2,1,0:T(8,128)(2,1)}, u32[]{:S(2)}) copy-start(bf16[1,128,512]{2,1,0:T(8,128)(2,1)} %param.9) | copy-start | bytes 393220
Sparse Core Ops, SparseCore 0:
  11.4 113.5 all-gather.8
  127.0 73.0 all-gather.6
  202.2 89.5 all-gather.4
  296.5 153.7 reduce-scatter.1
where the time goes:
time: 462 us; the launch traced here: 459 us
  waiting for transfers between devices  423 us (92%)
  between operations  13.8 us (3%)
  matrix products  11.5 us (2%)
  other arithmetic  9.42 us (2%)
    reduce_scatter x1, waiting for transfers between devices, per_device(): lax.psum_scatter((lax.dot_general(columns, key_grad, (((0,), (0,)), ((),...  150 us
    all_gather x1, waiting for transfers between devices, per_device(): lax.all_gather(local_weight, 'fsdp', axis=0, tiled=True)  115 us
    all_gather x1, waiting for transfers between devices, per_device(): lax.all_gather(weight, 'rep', axis=0, tiled=True)  91.7 us
    all_gather x1, waiting for transfers between devices, per_device(): lax.all_gather(momentum, 'rep', axis=0, tiled=True)  63.6 us
  transfers between devices with their start and end apart: 4, of which 4 were waited for; matrix products, arithmetic and copies ran while one was open for 4% of the time, Pallas kernels for 0%

commit v1 on v0

v1 whole, which is shorter than its diff:
```python
import jax
import jax.numpy as jnp
from jax import lax
from jax.experimental import pallas as pl
from jax.experimental.pallas import tpu as pltpu
from jax.sharding import PartitionSpec as P

epsilon = 1e-05
momentum_decay = 0.9
outer_rate = 0.7

D = 4096
K = 512
B = 512
H = 256
NB = D // B
SCALE = float(D) ** (-0.5)
F32 = jnp.float32
BF16 = jnp.bfloat16
VMEM = pl.BlockSpec(memory_space=pltpu.VMEM)
SMEM = pl.BlockSpec(memory_space=pltpu.SMEM)
PARAMS = pltpu.CompilerParams(vmem_limit_bytes=40 << 20)


def columns(place, slot):
    return pl.ds(pl.multiple_of(place[slot] * B, B), B)


def norm_kernel(place, tok, gain, cot, normed, send, inverse):
    total = jnp.zeros((tok.shape[0], 1), F32)
    for j in range(NB):
        part = tok[:, j * B : (j + 1) * B].astype(F32)
        total += jnp.sum(part * part, axis=1, keepdims=True)
    scale = lax.rsqrt(total * (1.0 / D) + epsilon)
    inverse[...] = scale
    for j in range(NB):
        where = columns(place, j)
        value = (tok[:, where].astype(F32) * scale * gain[:, where].astype(F32)).astype(BF16)
        normed[j] = value
        if j >= 5:
            send[:, (7 - j) * B : (8 - j) * B] = value
    send[:, 3 * B : 4 * B] = cot[...]
    other = pl.multiple_of((1 - place[NB]) * H, H)
    send[:, 4 * B : 4 * B + H] = normed[4, :, pl.ds(other, H)]


def outer(a, b):
    return lax.dot_general(a, b, (((0,), (0,)), ((), ())), preferred_element_type=F32)


def grad_kernel(place, normed, cot, got, half, terms, own):
    mine = cot[...]
    theirs = got[:, 3 * B : 4 * B]
    here = pl.multiple_of(place[NB] * H, H)
    half[...] = (
        (outer(normed[4, :, pl.ds(here, H)], mine) + outer(got[:, 4 * B : 4 * B + H], theirs)) * SCALE
    ).astype(BF16)
    for j in (3, 2, 1):
        terms[j - 1] = (
            outer(normed[j], mine) + outer(got[:, (j - 1) * B : j * B], theirs)
        ) * SCALE
    own[...] = outer(normed[0], mine) * SCALE


def token_kernel(
    place, tok, gain, inverse, normed, cot, w0, w1, w2, w3, h4, swapped, swapped4, keys, grad, w4, back
):
    here = pl.multiple_of(place[NB] * H, H)
    there = pl.multiple_of((1 - place[NB]) * H, H)
    w4[pl.ds(here, H), :] = h4[...]
    w4[pl.ds(there, H), :] = swapped4[...]
    blocks = (w0, w1, w2, w3, w4, swapped.at[2], swapped.at[1], swapped.at[0])
    mine = cot[...]
    total = jnp.zeros(keys.shape, F32)
    mixed = jnp.zeros((tok.shape[0], 1), F32)
    for j, block in enumerate(blocks):
        where = columns(place, j)
        w = block[...]
        total += jnp.dot(normed[j], w, preferred_element_type=F32)
        down = (
            lax.dot_general(mine, w, (((1,), (1,)), ((), ())), preferred_element_type=F32) * SCALE
        ).astype(BF16)
        back[j] = down
        up = down.astype(F32) * gain[:, where].astype(F32)
        mixed += jnp.sum(up * tok[:, where].astype(F32), axis=1, keepdims=True)
    keys[...] = (total * SCALE).astype(BF16)
    scale = inverse[...]
    factor = scale * scale * (mixed * (1.0 / D))
    for j in range(NB):
        where = columns(place, j)
        up = back[j].astype(F32) * gain[:, where].astype(F32)
        grad[:, where] = (scale * (up - tok[:, where].astype(F32) * factor)).astype(BF16)


def shape(dims, kind):
    return jax.ShapeDtypeStruct(dims, kind)


def per_device(tokens, norm_gain, weight, momentum, key_grad, matching):
    rows = tokens.shape[0]
    n = 32
    me = lax.axis_index("fsdp")
    z, y, core = me // 4, (me // 2) % 2, me % 2
    sign = 2 * core - 1
    place = jnp.concatenate([(z + sign * jnp.arange(NB) + NB) % NB, core[None]]).astype(jnp.int32)
    gain = norm_gain[None]

    def along(v, perm):
        return lax.ppermute(v, "fsdp", perm)

    swap_core = [(i, i ^ 1) for i in range(n)]
    swap_y = [(i, i ^ 2) for i in range(n)]
    sums_on = [(i, (i + (4 if i % 2 else -4)) % n) for i in range(n)]
    rows_on = [(i, (i - (4 if i % 2 else -4)) % n) for i in range(n)]

    r = lax.axis_index("rep")
    rx, ry = r // 4, r % 4
    both = jnp.concatenate([weight[0], momentum[0]], axis=0)
    from_x = [both] + [
        lax.ppermute(both, "rep", [(i, (i + 4 * k) % 16) for i in range(16)]) for k in (1, 2, 3)
    ]

    def wanted_by(row):
        source = lax.dynamic_index_in_dim(matching, row, 0, keepdims=False)
        k = (rx - source // 4 + 4) % 4
        return lax.select_n(k, *from_x)

    local = weight[0]
    other_y = along(local, swap_y)
    pair = jnp.where(y == 0, jnp.stack([local, other_y]), jnp.stack([other_y, local]))
    other_pair = along(pair, swap_core)
    w0 = jnp.where(
        core == 0,
        jnp.stack([pair, other_pair], axis=1),
        jnp.stack([other_pair, pair], axis=1),
    ).reshape(B, K)

    normed, send, inverse = pl.pallas_call(
        norm_kernel,
        out_shape=(
            shape((NB, rows, B), BF16),
            shape((rows, 4 * B + H), BF16),
            shape((rows, 1), F32),
        ),
        in_specs=[SMEM, VMEM, VMEM, VMEM],
        out_specs=(VMEM, VMEM, VMEM),
        compiler_params=PARAMS,
        name="norm",
    )(place, tokens, gain, key_grad)
    got = along(send, swap_core)
    half, terms, own = pl.pallas_call(
        grad_kernel,
        out_shape=(shape((H, K), BF16), shape((3, B, K), F32), shape((B, K), F32)),
        in_specs=[SMEM, VMEM, VMEM, VMEM],
        out_specs=(VMEM, VMEM, VMEM),
        compiler_params=PARAMS,
        name="weight_grad",
    )(place, normed, key_grad, got)

    w1 = along(w0, rows_on)
    s3 = along(half, sums_on)
    w2 = along(w1, rows_on)
    s3 = s3.astype(F32)
    nothing = jnp.zeros_like(s3)
    s3 = jnp.where(
        core == 0, jnp.concatenate([s3, nothing], axis=0), jnp.concatenate([nothing, s3], axis=0)
    )
    s2 = along((terms[2] + s3).astype(BF16), sums_on)
    w3 = along(w2, rows_on)
    s1 = along((terms[1] + s2.astype(F32)).astype(BF16), sums_on)
    h4 = along(lax.dynamic_slice_in_dim(w3, core * H, H, 0), rows_on)
    s0 = along((terms[0] + s1.astype(F32)).astype(BF16), sums_on)
    swapped = along(jnp.stack([w1, w2, w3]), swap_core)
    swapped4 = along(h4, swap_core)

    keys, token_grad = pl.pallas_call(
        token_kernel,
        out_shape=(shape((rows, K), BF16), shape((rows, D), BF16)),
        in_specs=[SMEM] + [VMEM] * 12,
        out_specs=(VMEM, VMEM),
        scratch_shapes=[pltpu.VMEM((B, K), BF16), pltpu.VMEM((NB, rows, B), BF16)],
        compiler_params=PARAMS,
        name="token_grad",
    )(place, tokens, gain, inverse, normed, key_grad, w0, w1, w2, w3, h4, swapped, swapped4)

    total = (own + s0.astype(F32)).reshape(2, 2, B // 4, K)
    theirs = lax.dynamic_index_in_dim(total, 1 - core, 1, keepdims=False).astype(BF16)
    total = lax.dynamic_index_in_dim(total, core, 1, keepdims=False) + along(
        theirs, swap_core
    ).astype(F32)
    theirs = lax.dynamic_index_in_dim(total, 1 - y, 0, keepdims=False).astype(BF16)
    grad = lax.dynamic_index_in_dim(total, y, 0, keepdims=False) + along(theirs, swap_y).astype(F32)
    grad = grad.astype(BF16).astype(F32)

    from_y = [wanted_by(r)]
    for m in (1, 2, 3):
        target = rx * 4 + (ry + m) % 4
        from_y.append(
            lax.ppermute(
                wanted_by(target), "rep", [(i, i // 4 * 4 + (i + m) % 4) for i in range(16)]
            )
        )
    source = lax.dynamic_index_in_dim(matching, r, 0, keepdims=False)
    partner = lax.select_n((ry - source % 4 + 4) % 4, *from_y).astype(F32)
    mean = (both.astype(F32) + partner) * 0.5
    rows_w = weight.shape[1]
    mean_weight, mean_momentum = mean[:rows_w], mean[rows_w:]
    momentum_next = momentum_decay * mean_momentum + grad
    new_weight = (mean_weight - outer_rate * (grad + momentum_decay * momentum_next)).astype(BF16)
    return (keys, token_grad, new_weight[None], momentum_next.astype(BF16)[None])


def solution(mesh):
    in_specs = (
        P(("rep", "fsdp"), None),
        P(),
        P("rep", "fsdp", None),
        P("rep", "fsdp", None),
        P(("rep", "fsdp"), None),
        P(),
    )
    out_specs = (
        P(("rep", "fsdp"), None),
        P(("rep", "fsdp"), None),
        P("rep", "fsdp", None),
        P("rep", "fsdp", None),
    )
    return jax.shard_map(
        per_device, mesh=mesh, in_specs=in_specs, out_specs=out_specs, check_vma=False
    )
```

time: 462 us -> 162 us (0.35)
  the two profiles are of different devices: /device:TPU:1 before, /device:TPU:43 now
where the time goes in v1:
time: 162 us; the launch traced here: 161 us
  starting transfers between devices  71.8 us (44%)
  waiting for transfers between devices  46.6 us (29%)
  other arithmetic  13.2 us (8%)
  between operations  11.7 us (7%)
  Pallas kernels  11 us (7%)
  local copies, waits for them, and re-layouts  6.66 us (4%)
    ppermute x15, starting transfers between devices, along(): return lax.ppermute(v, 'fsdp', perm)  52.7 us
    ppermute x15, waiting for transfers between devices, along(): return lax.ppermute(v, 'fsdp', perm)  26.5 us
    ppermute x3, waiting for transfers between devices, per_device(): lax.ppermute(wanted_by(target), 'rep', [(i, i // 4 * 4 + (i + m) % 4) for...  20.2 us
    ppermute x3, starting transfers between devices, per_device(): lax.ppermute(both, 'rep', [(i, (i + 4 * k) % 16) for i in range(16)])  10.2 us
    ppermute x3, starting transfers between devices, per_device(): lax.ppermute(wanted_by(target), 'rep', [(i, i // 4 * 4 + (i + m) % 4) for...  8.88 us
    pallas_call x1, Pallas kernels, per_device(): pl.pallas_call(token_kernel, out_shape=(shape((rows, K), BF16), shape((ro...  5.68 us
    unnamed x30, local copies, waits for them, and re-layouts  5.14 us
  transfers between devices with their start and end apart: 21, of which 7 were waited for; matrix products, arithmetic and copies ran while one was open for 9% of the time, Pallas kernels for 2%

profile of v1, /device:TPU:43, one launch (start us, length us, event | category | flops | bytes accessed | tf_op | source)
XLA Modules:
  0.0 161.0 jit_solution(807502364995863013)
XLA Ops:
  0.7 0.7 broadcast_in_dim.14.gain
  1.5 1.5 copy-done
  3.0 0.9 copy-done.4
  4.0 2.7 %norm.1 = (bf16[8,240,512]{2,1,0:T(8,128)(2,1)S(1)}, bf16[240,2304]{1,0:T(8,128)(2,1)}, f32[240,1]{1,0:T(8,128)S(1)}) custom-call(s32[9]{0:T(128)S(1)} %pad_add_fusion.place, bf16[240,4096]{1,0:T(8,128)(2,1)S(1)} %copy-done, bf16[1,4096]{1,0:T(2,128)(2,1)S(1)} %broadcast_in_dim.14.gain, bf16[240,512]{1,0:T(8,128)(2,1)S(1)} %copy-done.4), custom_call_target="tpu_custom_call" | custom-call | tf_op jit(solution)/shard_map/norm/pallas_call | solution.py:138
  6.7 2.6 %collective-permute-start.14 = (bf16[240,2304]{1,0:T(8,128)(2,1)}, bf16[240,2304]{1,0:T(8,128)(2,1)}, u32[]{:S(2)}, u32[]{:S(2)}) collective-permute-start(bf16[240,2304]{1,0:T(8,128)(2,1)} %get-tuple-element.16), channel_id=1, source_target_pairs={{0,1},{1,0},{2,3},{3,2},{4,5},{5,4},{6,7},{7,6},{8,9},{9,8},{10,11... | collective-permute-start | bytes 3317768 | tf_op jit(solution)/shard_map/ppermute | solution.py:109
  9.3 2.6 %collective-permute-start = (bf16[128,512]{1,0:T(8,128)(2,1)S(1)}, bf16[128,512]{1,0:T(8,128)(2,1)S(1)}, u32[]{:S(2)}, u32[]{:S(2)}) collective-permute-start(bf16[128,512]{1,0:T(8,128)(2,1)S(1)} %bitcast.51), channel_id=1, source_target_pairs={{0,2},{1,3},{2,0},{3,1},{4,6},{5,7},{6,4},{7,5},{8,10},{9,11},{10,... | collective-permute-start | bytes 393224 | tf_op jit(solution)/shard_map/ppermute | solution.py:109
  12.0 11.1 %collective-permute-done = bf16[128,512]{1,0:T(8,128)(2,1)S(1)} collective-permute-done((bf16[128,512]{1,0:T(8,128)(2,1)S(1)}, bf16[128,512]{1,0:T(8,128)(2,1)S(1)}, u32[]{:S(2)}, u32[]{:S(2)}) %collective-permute-start) | collective-permute-done | bytes 131104 | tf_op jit(solution)/shard_map/ppermute | solution.py:109
  23.0 0.7 maximum_select_fusion.2
  23.8 2.7 %collective-permute-start.1 = (bf16[2,128,512]{2,1,0:T(8,128)(2,1)}, bf16[2,128,512]{2,1,0:T(8,128)(2,1)}, u32[]{:S(2)}, u32[]{:S(2)}) collective-permute-start(bf16[2,128,512]{2,1,0:T(8,128)(2,1)} %maximum_select_fusion.2), channel_id=1, source_target_pairs={{0,1},{1,0},{2,3},{3,2},{4,5},{5,4},{6,7},{7,6},{8,9},{9,8},{10,11... | collective-permute-start | bytes 786440 | tf_op jit(solution)/shard_map/ppermute | solution.py:109
  26.5 2.6 %weight_grad.1 = (bf16[256,512]{1,0:T(8,128)(2,1)}, f32[3,512,512]{2,1,0:T(8,128)S(1)}, f32[512,512]{1,0:T(8,128)S(1)}) custom-call(s32[9]{0:T(128)S(1)} %pad_add_fusion.place, bf16[8,240,512]{2,1,0:T(8,128)(2,1)S(1)} %get-tuple-element.13.normed, bf16[240,512]{1,0:T(8,128)(2,1)S(1)} %copy-done.5, bf16[240,2304]{1,0:T(8,128)(2,1)} %collective-permute-done.14.got), custom_call_target="tpu_custom_call" | custom-call | tf_op jit(solution)/shard_map/weight_grad/pallas_call | solution.py:151
  29.1 1.6 %copy-done.2 = f32[3,512,512]{2,1,0:T(8,128)} copy-done((f32[3,512,512]{2,1,0:T(8,128)}, f32[3,512,512]{2,1,0:T(8,128)S(1)}, u32[]{:S(2)}) %copy-start.2) | copy-done | bytes 3145752
  30.7 1.0 copy-done.8
  31.7 4.0 %collective-permute-start.15 = (bf16[256,512]{1,0:T(8,128)(2,1)}, bf16[256,512]{1,0:T(8,128)(2,1)}, u32[]{:S(2)}, u32[]{:S(2)}) collective-permute-start(bf16[256,512]{1,0:T(8,128)(2,1)} %get-tuple-element.19), channel_id=1, source_target_pairs={{0,28},{1,5},{2,30},{3,7},{4,0},{5,9},{6,2},{7,11},{8,4},{9,13},{1... | collective-permute-start | bytes 786440 | tf_op jit(solution)/shard_map/ppermute | solution.py:109
  35.7 1.2 maximum_select_fusion.1
  36.8 1.2 maximum_select_fusion
  38.1 8.6 %collective-permute-start.2 = (bf16[512,512]{1,0:T(8,128)(2,1)S(1)}, bf16[512,512]{1,0:T(8,128)(2,1)S(1)}, u32[]{:S(2)}, u32[]{:S(2)}) collective-permute-start(bf16[512,512]{1,0:T(8,128)(2,1)S(1)} %bitcast.48), channel_id=1, source_target_pairs={{0,4},{1,29},{2,6},{3,31},{4,8},{5,1},{6,10},{7,3},{8,12},{9,5},{1... | collective-permute-start | bytes 1572872 | tf_op jit(solution)/shard_map/ppermute | solution.py:109
  46.7 1.0 convert_element_type.59
  47.9 1.9 %collective-permute-start.16 = (bf16[512,512]{1,0:T(8,128)(2,1)S(1)}, bf16[512,512]{1,0:T(8,128)(2,1)S(1)}, u32[]{:S(2)}, u32[]{:S(2)}) collective-permute-start(bf16[512,512]{1,0:T(8,128)(2,1)S(1)} %fusion), channel_id=1, source_target_pairs={{0,28},{1,5},{2,30},{3,7},{4,0},{5,9},{6,2},{7,11},{8,4},{9,13},{1... | collective-permute-start | bytes 1572872 | tf_op jit(solution)/shard_map/ppermute | solution.py:109
  49.8 2.9 %collective-permute-done.2.w1 = bf16[512,512]{1,0:T(8,128)(2,1)S(1)} collective-permute-done((bf16[512,512]{1,0:T(8,128)(2,1)S(1)}, bf16[512,512]{1,0:T(8,128)(2,1)S(1)}, u32[]{:S(2)}, u32[]{:S(2)}) %collective-permute-start.2) | collective-permute-done | bytes 524320 | tf_op jit(solution)/shard_map/ppermute | solution.py:109
  52.8 5.0 %collective-permute-start.3 = (bf16[512,512]{1,0:T(8,128)(2,1)S(1)}, bf16[512,512]{1,0:T(8,128)(2,1)}, u32[]{:S(2)}, u32[]{:S(2)}) collective-permute-start(bf16[512,512]{1,0:T(8,128)(2,1)S(1)} %collective-permute-done.2.w1), channel_id=1, source_target_pairs={{0,4},{1,29},{2,6},{3,31},{4,8},{5,1},{6,10},{7,3},{8,12},{9,5},{1... | collective-permute-start | bytes 1572872 | tf_op jit(solution)/shard_map/ppermute | solution.py:109
  57.8 4.4 %collective-permute-done.16 = bf16[512,512]{1,0:T(8,128)(2,1)S(1)} collective-permute-done((bf16[512,512]{1,0:T(8,128)(2,1)S(1)}, bf16[512,512]{1,0:T(8,128)(2,1)S(1)}, u32[]{:S(2)}, u32[]{:S(2)}) %collective-permute-start.16) | collective-permute-done | bytes 524320 | tf_op jit(solution)/shard_map/ppermute | solution.py:109
  62.5 2.1 %collective-permute-start.17 = (bf16[512,512]{1,0:T(8,128)(2,1)S(1)}, bf16[512,512]{1,0:T(8,128)(2,1)S(1)}, u32[]{:S(2)}, u32[]{:S(2)}) collective-permute-start(bf16[512,512]{1,0:T(8,128)(2,1)S(1)} %fusion.1), channel_id=1, source_target_pairs={{0,28},{1,5},{2,30},{3,7},{4,0},{5,9},{6,2},{7,11},{8,4},{9,13},{1... | collective-permute-start | bytes 1572872 | tf_op jit(solution)/shard_map/ppermute | solution.py:109
  64.5 1.0 collective-permute-done.3.w2
  65.5 5.1 %collective-permute-start.4 = (bf16[512,512]{1,0:T(8,128)(2,1)}, bf16[512,512]{1,0:T(8,128)(2,1)S(1)}, u32[]{:S(2)}, u32[]{:S(2)}) collective-permute-start(bf16[512,512]{1,0:T(8,128)(2,1)} %collective-permute-done.3.w2), channel_id=1, source_target_pairs={{0,4},{1,29},{2,6},{3,31},{4,8},{5,1},{6,10},{7,3},{8,12},{9,5},{1... | collective-permute-start | bytes 1572872 | tf_op jit(solution)/shard_map/ppermute | solution.py:109
  70.6 7.0 %collective-permute-done.17 = bf16[512,512]{1,0:T(8,128)(2,1)S(1)} collective-permute-done((bf16[512,512]{1,0:T(8,128)(2,1)S(1)}, bf16[512,512]{1,0:T(8,128)(2,1)S(1)}, u32[]{:S(2)}, u32[]{:S(2)}) %collective-permute-start.17) | collective-permute-done | bytes 524320 | tf_op jit(solution)/shard_map/ppermute | solution.py:109
  77.6 1.0 fusion.2
  78.6 1.9 %collective-permute-start.18 = (bf16[512,512]{1,0:T(8,128)(2,1)}, bf16[512,512]{1,0:T(8,128)(2,1)}, u32[]{:S(2)}, u32[]{:S(2)}) collective-permute-start(bf16[512,512]{1,0:T(8,128)(2,1)} %fusion.2), channel_id=1, source_target_pairs={{0,28},{1,5},{2,30},{3,7},{4,0},{5,9},{6,2},{7,11},{8,4},{9,13},{1... | collective-permute-start | bytes 1572872 | tf_op jit(solution)/shard_map/ppermute | solution.py:109
  80.6 0.7 pad_maximum_fusion.1
  81.3 2.2 %collective-permute-start.10 = (bf16[256,512]{1,0:T(8,128)(2,1)}, bf16[256,512]{1,0:T(8,128)(2,1)}, u32[]{:S(2)}, u32[]{:S(2)}) collective-permute-start(bf16[256,512]{1,0:T(8,128)(2,1)} %pad_maximum_fusion.1), channel_id=1, source_target_pairs={{0,384},{32,416},{64,448},{96,480},{128,0},{160,32},{192,64},{224,... | collective-permute-start | bytes 786440 | tf_op jit(solution)/shard_map/ppermute | solution.py:120
  83.5 3.1 %collective-permute-start.8 = (bf16[256,512]{1,0:T(8,128)(2,1)}, bf16[256,512]{1,0:T(8,128)(2,1)}, u32[]{:S(2)}, u32[]{:S(2)}) collective-permute-start(bf16[256,512]{1,0:T(8,128)(2,1)} %pad_maximum_fusion.1), channel_id=1, source_target_pairs={{0,128},{32,160},{64,192},{96,224},{128,256},{160,288},{192,320},{... | collective-permute-start | bytes 786440 | tf_op jit(solution)/shard_map/ppermute | solution.py:120
  86.6 5.0 %collective-permute-start.9 = (bf16[256,512]{1,0:T(8,128)(2,1)}, bf16[256,512]{1,0:T(8,128)(2,1)}, u32[]{:S(2)}, u32[]{:S(2)}) collective-permute-start(bf16[256,512]{1,0:T(8,128)(2,1)} %pad_maximum_fusion.1), channel_id=1, source_target_pairs={{0,256},{32,288},{64,320},{96,352},{128,384},{160,416},{192,448},{... | collective-permute-start | bytes 786440 | tf_op jit(solution)/shard_map/ppermute | solution.py:120
  102.8 1.5 pad_maximum_fusion
  104.2 6.9 %collective-permute-start.6 = (bf16[3,512,512]{2,1,0:T(8,128)(2,1)S(1)}, bf16[3,512,512]{2,1,0:T(8,128)(2,1)S(1)}, u32[]{:S(2)}, u32[]{:S(2)}) collective-permute-start(bf16[3,512,512]{2,1,0:T(8,128)(2,1)S(1)} %pad_maximum_fusion), channel_id=1, source_target_pairs={{0,1},{1,0},{2,3},{3,2},{4,5},{5,4},{6,7},{7,6},{8,9},{9,8},{10,11... | collective-permute-start | bytes 4718600 | tf_op jit(solution)/shard_map/ppermute | solution.py:109
  111.2 1.2 convert_add_fusion
  112.5 1.9 %collective-permute-start.19 = (bf16[2,128,512]{2,1,0:T(8,128)(2,1)S(1)}, bf16[2,128,512]{2,1,0:T(8,128)(2,1)S(1)}, u32[]{:S(2)}, u32[]{:S(2)}) collective-permute-start(bf16[2,128,512]{2,1,0:T(8,128)(2,1)S(1)} %fusion.6), channel_id=1, source_target_pairs={{0,1},{1,0},{2,3},{3,2},{4,5},{5,4},{6,7},{7,6},{8,9},{9,8},{10,11... | collective-permute-start | bytes 786440 | tf_op jit(solution)/shard_map/ppermute | solution.py:109
  114.4 1.4 select_select_fusion.2
  115.8 2.2 %collective-permute-start.11 = (bf16[256,512]{1,0:T(8,128)(2,1)S(1)}, bf16[256,512]{1,0:T(8,128)(2,1)S(1)}, u32[]{:S(2)}, u32[]{:S(2)}) collective-permute-start(bf16[256,512]{1,0:T(8,128)(2,1)S(1)} %get-tuple-element.22), channel_id=1, source_target_pairs={{0,32},{32,64},{64,96},{96,0},{128,160},{160,192},{192,224},{224,1... | collective-permute-start | bytes 786440 | tf_op jit(solution)/shard_map/ppermute | solution.py:199
  118.0 4.8 %collective-permute-start.12 = (bf16[256,512]{1,0:T(8,128)(2,1)S(1)}, bf16[256,512]{1,0:T(8,128)(2,1)S(1)}, u32[]{:S(2)}, u32[]{:S(2)}) collective-permute-start(bf16[256,512]{1,0:T(8,128)(2,1)S(1)} %get-tuple-element.24), channel_id=1, source_target_pairs={{0,64},{32,96},{64,0},{96,32},{128,192},{160,224},{192,128},{224,1... | collective-permute-start | bytes 786440 | tf_op jit(solution)/shard_map/ppermute | solution.py:199
  122.8 1.9 %collective-permute-start.13 = (bf16[256,512]{1,0:T(8,128)(2,1)S(1)}, bf16[256,512]{1,0:T(8,128)(2,1)S(1)}, u32[]{:S(2)}, u32[]{:S(2)}) collective-permute-start(bf16[256,512]{1,0:T(8,128)(2,1)S(1)} %get-tuple-element.23), channel_id=1, source_target_pairs={{0,96},{32,0},{64,32},{96,64},{128,224},{160,128},{192,160},{224,1... | collective-permute-start | bytes 786440 | tf_op jit(solution)/shard_map/ppermute | solution.py:199
  124.8 1.9 %collective-permute-start.5 = (bf16[256,512]{1,0:T(8,128)(2,1)S(1)}, bf16[256,512]{1,0:T(8,128)(2,1)S(1)}, u32[]{:S(2)}, u32[]{:S(2)}) collective-permute-start(bf16[256,512]{1,0:T(8,128)(2,1)S(1)} %constant_dynamic-slice_fusion), channel_id=1, source_target_pairs={{0,4},{1,29},{2,6},{3,31},{4,8},{5,1},{6,10},{7,3},{8,12},{9,5},{1... | collective-permute-start | bytes 786440 | tf_op jit(solution)/shard_map/ppermute | solution.py:109
  126.8 3.1 %collective-permute-start.20 = (bf16[128,512]{1,0:T(8,128)(2,1)S(1)}, bf16[128,512]{1,0:T(8,128)(2,1)S(1)}, u32[]{:S(2)}, u32[]{:S(2)}) collective-permute-start(bf16[128,512]{1,0:T(8,128)(2,1)S(1)} %fusion.10), channel_id=1, source_target_pairs={{0,2},{1,3},{2,0},{3,1},{4,6},{5,7},{6,4},{7,5},{8,10},{9,11},{10,... | collective-permute-start | bytes 393224 | tf_op jit(solution)/shard_map/ppermute | solution.py:109
  130.0 14.5 %collective-permute-done.12 = bf16[256,512]{1,0:T(8,128)(2,1)S(1)} collective-permute-done((bf16[256,512]{1,0:T(8,128)(2,1)S(1)}, bf16[256,512]{1,0:T(8,128)(2,1)S(1)}, u32[]{:S(2)}, u32[]{:S(2)}) %collective-permute-start.12) | collective-permute-done | bytes 262176 | tf_op jit(solution)/shard_map/ppermute | solution.py:199
  144.5 5.7 %collective-permute-done.13 = bf16[256,512]{1,0:T(8,128)(2,1)S(1)} collective-permute-done((bf16[256,512]{1,0:T(8,128)(2,1)S(1)}, bf16[256,512]{1,0:T(8,128)(2,1)S(1)}, u32[]{:S(2)}, u32[]{:S(2)}) %collective-permute-start.13) | collective-permute-done | bytes 262176 | tf_op jit(solution)/shard_map/ppermute | solution.py:199
  150.1 1.3 add_multiply_fusion
  151.4 2.4 %collective-permute-start.7 = (bf16[256,512]{1,0:T(8,128)(2,1)S(1)}, bf16[256,512]{1,0:T(8,128)(2,1)S(1)}, u32[]{:S(2)}, u32[]{:S(2)}) collective-permute-start(bf16[256,512]{1,0:T(8,128)(2,1)S(1)} %collective-permute-done.5.h4), channel_id=1, source_target_pairs={{0,1},{1,0},{2,3},{3,2},{4,5},{5,4},{6,7},{7,6},{8,9},{9,8},{10,11... | collective-permute-start | bytes 786440 | tf_op jit(solution)/shard_map/ppermute | solution.py:109
  153.8 0.7 fusion.9
  154.6 0.7 fusion.11
  155.3 5.7 %token_grad.1 = (bf16[240,512]{1,0:T(8,128)(2,1)}, bf16[240,4096]{1,0:T(8,128)(2,1)}) custom-call(s32[9]{0:T(128)S(1)} %pad_add_fusion.place, bf16[240,4096]{1,0:T(8,128)(2,1)S(1)} %copy-done.1, bf16[1,4096]{1,0:T(2,128)(2,1)S(1)} %broadcast_in_dim.14.gain, f32[240,1]{1,0:T(8,128)S(1)} %get-tuple-element.12.inverse, ...), custom_call_target="tpu_custom_call" | custom-call | tf_op jit(solution)/shard_map/token_grad/pallas_call | solution.py:176
  (50 shorter events, 1.5 us)
Async XLA Ops:
  1.5 1.5 copy-start
  3.0 0.9 copy-start.4
  4.0 5.3 %copy-start.10 = (bf16[1,128,512]{2,1,0:T(8,128)(2,1)S(1)}, bf16[1,128,512]{2,1,0:T(8,128)(2,1)}, u32[]{:S(2)}) copy-start(bf16[1,128,512]{2,1,0:T(8,128)(2,1)} %param.8) | copy-start | bytes 393220
  4.0 22.5 %copy-start.5 = (bf16[240,512]{1,0:T(8,128)(2,1)S(1)}, bf16[240,512]{1,0:T(8,128)(2,1)}, u32[]{:S(2)}) copy-start(bf16[240,512]{1,0:T(8,128)(2,1)} %cot.5) | copy-start | bytes 737284
  6.7 19.8 %collective-permute-start.14 = (bf16[240,2304]{1,0:T(8,128)(2,1)}, bf16[240,2304]{1,0:T(8,128)(2,1)}, u32[]{:S(2)}, u32[]{:S(2)}) collective-permute-start(bf16[240,2304]{1,0:T(8,128)(2,1)} %get-tuple-element.16), channel_id=1, source_target_pairs={{0,1},{1,0},{2,3},{3,2},{4,5},{5,4},{6,7},{7,6},{8,9},{9,8},{10,11... | collective-permute-start | bytes 3317768 | tf_op jit(solution)/shard_map/ppermute | solution.py:109
  9.3 13.7 %collective-permute-start = (bf16[128,512]{1,0:T(8,128)(2,1)S(1)}, bf16[128,512]{1,0:T(8,128)(2,1)S(1)}, u32[]{:S(2)}, u32[]{:S(2)}) collective-permute-start(bf16[128,512]{1,0:T(8,128)(2,1)S(1)} %bitcast.51), channel_id=1, source_target_pairs={{0,2},{1,3},{2,0},{3,1},{4,6},{5,7},{6,4},{7,5},{8,10},{9,11},{10,... | collective-permute-start | bytes 393224 | tf_op jit(solution)/shard_map/ppermute | solution.py:109
  23.0 3.4 %copy-start.13 = (bf16[128,512]{1,0:T(8,128)(2,1)}, bf16[128,512]{1,0:T(8,128)(2,1)S(1)}, u32[]{:S(2)}) copy-start(bf16[128,512]{1,0:T(8,128)(2,1)S(1)} %collective-permute-done) | copy-start | bytes 393220
  23.8 13.1 %collective-permute-start.1 = (bf16[2,128,512]{2,1,0:T(8,128)(2,1)}, bf16[2,128,512]{2,1,0:T(8,128)(2,1)}, u32[]{:S(2)}, u32[]{:S(2)}) collective-permute-start(bf16[2,128,512]{2,1,0:T(8,128)(2,1)} %maximum_select_fusion.2), channel_id=1, source_target_pairs={{0,1},{1,0},{2,3},{3,2},{4,5},{5,4},{6,7},{7,6},{8,9},{9,8},{10,11... | collective-permute-start | bytes 786440 | tf_op jit(solution)/shard_map/ppermute | solution.py:109
  29.1 1.6 %copy-start.2 = (f32[3,512,512]{2,1,0:T(8,128)}, f32[3,512,512]{2,1,0:T(8,128)S(1)}, u32[]{:S(2)}) copy-start(f32[3,512,512]{2,1,0:T(8,128)S(1)} %get-tuple-element.18) | copy-start | bytes 9437188
  30.7 1.0 copy-start.8
  31.7 15.0 %collective-permute-start.15 = (bf16[256,512]{1,0:T(8,128)(2,1)}, bf16[256,512]{1,0:T(8,128)(2,1)}, u32[]{:S(2)}, u32[]{:S(2)}) collective-permute-start(bf16[256,512]{1,0:T(8,128)(2,1)} %get-tuple-element.19), channel_id=1, source_target_pairs={{0,28},{1,5},{2,30},{3,7},{4,0},{5,9},{6,2},{7,11},{8,4},{9,13},{1... | collective-permute-start | bytes 786440 | tf_op jit(solution)/shard_map/ppermute | solution.py:109
  35.7 12.0 %copy-start.3 = (f32[3,512,512]{2,1,0:T(8,128)S(1)}, f32[3,512,512]{2,1,0:T(8,128)}, u32[]{:S(2)}) copy-start(f32[3,512,512]{2,1,0:T(8,128)} %copy-done.2) | copy-start | bytes 9437188
  38.1 14.7 %collective-permute-start.2 = (bf16[512,512]{1,0:T(8,128)(2,1)S(1)}, bf16[512,512]{1,0:T(8,128)(2,1)S(1)}, u32[]{:S(2)}, u32[]{:S(2)}) collective-permute-start(bf16[512,512]{1,0:T(8,128)(2,1)S(1)} %bitcast.48), channel_id=1, source_target_pairs={{0,4},{1,29},{2,6},{3,31},{4,8},{5,1},{6,10},{7,3},{8,12},{9,5},{1... | collective-permute-start | bytes 1572872 | tf_op jit(solution)/shard_map/ppermute | solution.py:109
  47.9 14.3 %collective-permute-start.16 = (bf16[512,512]{1,0:T(8,128)(2,1)S(1)}, bf16[512,512]{1,0:T(8,128)(2,1)S(1)}, u32[]{:S(2)}, u32[]{:S(2)}) collective-permute-start(bf16[512,512]{1,0:T(8,128)(2,1)S(1)} %fusion), channel_id=1, source_target_pairs={{0,28},{1,5},{2,30},{3,7},{4,0},{5,9},{6,2},{7,11},{8,4},{9,13},{1... | collective-permute-start | bytes 1572872 | tf_op jit(solution)/shard_map/ppermute | solution.py:109
  52.8 11.8 %copy-start.6 = (bf16[512,512]{1,0:T(8,128)(2,1)}, bf16[512,512]{1,0:T(8,128)(2,1)S(1)}, u32[]{:S(2)}) copy-start(bf16[512,512]{1,0:T(8,128)(2,1)S(1)} %collective-permute-done.2.w1) | copy-start | bytes 1572868
  52.8 12.7 %collective-permute-start.3 = (bf16[512,512]{1,0:T(8,128)(2,1)S(1)}, bf16[512,512]{1,0:T(8,128)(2,1)}, u32[]{:S(2)}, u32[]{:S(2)}) collective-permute-start(bf16[512,512]{1,0:T(8,128)(2,1)S(1)} %collective-permute-done.2.w1), channel_id=1, source_target_pairs={{0,4},{1,29},{2,6},{3,31},{4,8},{5,1},{6,10},{7,3},{8,12},{9,5},{1... | collective-permute-start | bytes 1572872 | tf_op jit(solution)/shard_map/ppermute | solution.py:109
  62.4 18.1 %copy-start.11 = (bf16[1,128,512]{2,1,0:T(8,128)(2,1)S(1)}, bf16[1,128,512]{2,1,0:T(8,128)(2,1)}, u32[]{:S(2)}) copy-start(bf16[1,128,512]{2,1,0:T(8,128)(2,1)} %param.9) | copy-start | bytes 393220
  62.5 29.2 %copy-start.14 = (s32[16]{0:T(128)S(1)}, s32[16]{0:T(128)}, u32[]{:S(2)}) copy-start(s32[16]{0:T(128)} %param.11) | copy-start | bytes 196
  62.5 15.2 %collective-permute-start.17 = (bf16[512,512]{1,0:T(8,128)(2,1)S(1)}, bf16[512,512]{1,0:T(8,128)(2,1)S(1)}, u32[]{:S(2)}, u32[]{:S(2)}) collective-permute-start(bf16[512,512]{1,0:T(8,128)(2,1)S(1)} %fusion.1), channel_id=1, source_target_pairs={{0,28},{1,5},{2,30},{3,7},{4,0},{5,9},{6,2},{7,11},{8,4},{9,13},{1... | collective-permute-start | bytes 1572872 | tf_op jit(solution)/shard_map/ppermute | solution.py:109
  65.5 37.2 %collective-permute-start.4 = (bf16[512,512]{1,0:T(8,128)(2,1)}, bf16[512,512]{1,0:T(8,128)(2,1)S(1)}, u32[]{:S(2)}, u32[]{:S(2)}) collective-permute-start(bf16[512,512]{1,0:T(8,128)(2,1)} %collective-permute-done.3.w2), channel_id=1, source_target_pairs={{0,4},{1,29},{2,6},{3,31},{4,8},{5,1},{6,10},{7,3},{8,12},{9,5},{1... | collective-permute-start | bytes 1572872 | tf_op jit(solution)/shard_map/ppermute | solution.py:109
  78.6 32.5 %collective-permute-start.18 = (bf16[512,512]{1,0:T(8,128)(2,1)}, bf16[512,512]{1,0:T(8,128)(2,1)}, u32[]{:S(2)}, u32[]{:S(2)}) collective-permute-start(bf16[512,512]{1,0:T(8,128)(2,1)} %fusion.2), channel_id=1, source_target_pairs={{0,28},{1,5},{2,30},{3,7},{4,0},{5,9},{6,2},{7,11},{8,4},{9,13},{1... | collective-permute-start | bytes 1572872 | tf_op jit(solution)/shard_map/ppermute | solution.py:109
  81.3 33.1 %collective-permute-start.10 = (bf16[256,512]{1,0:T(8,128)(2,1)}, bf16[256,512]{1,0:T(8,128)(2,1)}, u32[]{:S(2)}, u32[]{:S(2)}) collective-permute-start(bf16[256,512]{1,0:T(8,128)(2,1)} %pad_maximum_fusion.1), channel_id=1, source_target_pairs={{0,384},{32,416},{64,448},{96,480},{128,0},{160,32},{192,64},{224,... | collective-permute-start | bytes 786440 | tf_op jit(solution)/shard_map/ppermute | solution.py:120
  83.5 30.9 %collective-permute-start.8 = (bf16[256,512]{1,0:T(8,128)(2,1)}, bf16[256,512]{1,0:T(8,128)(2,1)}, u32[]{:S(2)}, u32[]{:S(2)}) collective-permute-start(bf16[256,512]{1,0:T(8,128)(2,1)} %pad_maximum_fusion.1), channel_id=1, source_target_pairs={{0,128},{32,160},{64,192},{96,224},{128,256},{160,288},{192,320},{... | collective-permute-start | bytes 786440 | tf_op jit(solution)/shard_map/ppermute | solution.py:120
  86.6 27.8 %collective-permute-start.9 = (bf16[256,512]{1,0:T(8,128)(2,1)}, bf16[256,512]{1,0:T(8,128)(2,1)}, u32[]{:S(2)}, u32[]{:S(2)}) collective-permute-start(bf16[256,512]{1,0:T(8,128)(2,1)} %pad_maximum_fusion.1), channel_id=1, source_target_pairs={{0,256},{32,288},{64,320},{96,352},{128,384},{160,416},{192,448},{... | collective-permute-start | bytes 786440 | tf_op jit(solution)/shard_map/ppermute | solution.py:120
  102.8 8.4 %copy-start.9 = (f32[512,512]{1,0:T(8,128)S(1)}, f32[512,512]{1,0:T(8,128)}, u32[]{:S(2)}) copy-start(f32[512,512]{1,0:T(8,128)} %copy-done.8) | copy-start | bytes 3145732
  104.2 51.1 %collective-permute-start.6 = (bf16[3,512,512]{2,1,0:T(8,128)(2,1)S(1)}, bf16[3,512,512]{2,1,0:T(8,128)(2,1)S(1)}, u32[]{:S(2)}, u32[]{:S(2)}) collective-permute-start(bf16[3,512,512]{2,1,0:T(8,128)(2,1)S(1)} %pad_maximum_fusion), channel_id=1, source_target_pairs={{0,1},{1,0},{2,3},{3,2},{4,5},{5,4},{6,7},{7,6},{8,9},{9,8},{10,11... | collective-permute-start | bytes 4718600 | tf_op jit(solution)/shard_map/ppermute | solution.py:109
  111.2 3.2 %copy-start.12 = (bf16[1,128,512]{2,1,0:T(8,128)(2,1)S(1)}, bf16[1,128,512]{2,1,0:T(8,128)(2,1)}, u32[]{:S(2)}) copy-start(bf16[1,128,512]{2,1,0:T(8,128)(2,1)} %param.9) | copy-start | bytes 393220
  112.5 12.3 %collective-permute-start.19 = (bf16[2,128,512]{2,1,0:T(8,128)(2,1)S(1)}, bf16[2,128,512]{2,1,0:T(8,128)(2,1)S(1)}, u32[]{:S(2)}, u32[]{:S(2)}) collective-permute-start(bf16[2,128,512]{2,1,0:T(8,128)(2,1)S(1)} %fusion.6), channel_id=1, source_target_pairs={{0,1},{1,0},{2,3},{3,2},{4,5},{5,4},{6,7},{7,6},{8,9},{9,8},{10,11... | collective-permute-start | bytes 786440 | tf_op jit(solution)/shard_map/ppermute | solution.py:109
  115.8 11.0 %collective-permute-start.11 = (bf16[256,512]{1,0:T(8,128)(2,1)S(1)}, bf16[256,512]{1,0:T(8,128)(2,1)S(1)}, u32[]{:S(2)}, u32[]{:S(2)}) collective-permute-start(bf16[256,512]{1,0:T(8,128)(2,1)S(1)} %get-tuple-element.22), channel_id=1, source_target_pairs={{0,32},{32,64},{64,96},{96,0},{128,160},{160,192},{192,224},{224,1... | collective-permute-start | bytes 786440 | tf_op jit(solution)/shard_map/ppermute | solution.py:199
  118.0 26.4 %collective-permute-start.12 = (bf16[256,512]{1,0:T(8,128)(2,1)S(1)}, bf16[256,512]{1,0:T(8,128)(2,1)S(1)}, u32[]{:S(2)}, u32[]{:S(2)}) collective-permute-start(bf16[256,512]{1,0:T(8,128)(2,1)S(1)} %get-tuple-element.24), channel_id=1, source_target_pairs={{0,64},{32,96},{64,0},{96,32},{128,192},{160,224},{192,128},{224,1... | collective-permute-start | bytes 786440 | tf_op jit(solution)/shard_map/ppermute | solution.py:199
  122.8 27.3 %collective-permute-start.13 = (bf16[256,512]{1,0:T(8,128)(2,1)S(1)}, bf16[256,512]{1,0:T(8,128)(2,1)S(1)}, u32[]{:S(2)}, u32[]{:S(2)}) collective-permute-start(bf16[256,512]{1,0:T(8,128)(2,1)S(1)} %get-tuple-element.23), channel_id=1, source_target_pairs={{0,96},{32,0},{64,32},{96,64},{128,224},{160,128},{192,160},{224,1... | collective-permute-start | bytes 786440 | tf_op jit(solution)/shard_map/ppermute | solution.py:199
  124.8 26.6 %collective-permute-start.5 = (bf16[256,512]{1,0:T(8,128)(2,1)S(1)}, bf16[256,512]{1,0:T(8,128)(2,1)S(1)}, u32[]{:S(2)}, u32[]{:S(2)}) collective-permute-start(bf16[256,512]{1,0:T(8,128)(2,1)S(1)} %constant_dynamic-slice_fusion), channel_id=1, source_target_pairs={{0,4},{1,29},{2,6},{3,31},{4,8},{5,1},{6,10},{7,3},{8,12},{9,5},{1... | collective-permute-start | bytes 786440 | tf_op jit(solution)/shard_map/ppermute | solution.py:109
  126.8 28.5 %copy-start.1 = (bf16[240,4096]{1,0:T(8,128)(2,1)S(1)}, bf16[240,4096]{1,0:T(8,128)(2,1)}, u32[]{:S(2)}) copy-start(bf16[240,4096]{1,0:T(8,128)(2,1)} %tok.3) | copy-start | bytes 5898244
  126.8 28.5 %copy-start.7 = (bf16[512,512]{1,0:T(8,128)(2,1)S(1)}, bf16[512,512]{1,0:T(8,128)(2,1)}, u32[]{:S(2)}) copy-start(bf16[512,512]{1,0:T(8,128)(2,1)} %copy-done.6) | copy-start | bytes 1572868
  126.8 27.0 %collective-permute-start.20 = (bf16[128,512]{1,0:T(8,128)(2,1)S(1)}, bf16[128,512]{1,0:T(8,128)(2,1)S(1)}, u32[]{:S(2)}, u32[]{:S(2)}) collective-permute-start(bf16[128,512]{1,0:T(8,128)(2,1)S(1)} %fusion.10), channel_id=1, source_target_pairs={{0,2},{1,3},{2,0},{3,1},{4,6},{5,7},{6,4},{7,5},{8,10},{9,11},{10,... | collective-permute-start | bytes 393224 | tf_op jit(solution)/shard_map/ppermute | solution.py:109
  151.4 3.9 %collective-permute-start.7 = (bf16[256,512]{1,0:T(8,128)(2,1)S(1)}, bf16[256,512]{1,0:T(8,128)(2,1)S(1)}, u32[]{:S(2)}, u32[]{:S(2)}) collective-permute-start(bf16[256,512]{1,0:T(8,128)(2,1)S(1)} %collective-permute-done.5.h4), channel_id=1, source_target_pairs={{0,1},{1,0},{2,3},{3,2},{4,5},{5,4},{6,7},{7,6},{8,9},{9,8},{10,11... | collective-permute-start | bytes 786440 | tf_op jit(solution)/shard_map/ppermute | solution.py:109

commit v2 on v1

v2 whole, which is shorter than its diff:
```python
import functools

import jax
import jax.numpy as jnp
from jax import lax
from jax.experimental import pallas as pl
from jax.experimental.pallas import tpu as pltpu
from jax.sharding import PartitionSpec as P

epsilon = 1e-05
momentum_decay = 0.9
outer_rate = 0.7

D = 4096
K = 512
B = 512
H = 256
NB = D // B
SCALE = float(D) ** (-0.5)
F32 = jnp.float32
BF16 = jnp.bfloat16
VMEM = pl.BlockSpec(memory_space=pltpu.VMEM)
SMEM = pl.BlockSpec(memory_space=pltpu.SMEM)
ANY = pl.BlockSpec(memory_space=pl.ANY)


def columns(place, slot):
    return pl.ds(pl.multiple_of(place[slot] * B, B), B)


def norm_kernel(place, tok, gain, cot, normed, send, inverse):
    total = jnp.zeros((tok.shape[0], 1), F32)
    for j in range(NB):
        part = tok[:, j * B : (j + 1) * B].astype(F32)
        total += jnp.sum(part * part, axis=1, keepdims=True)
    scale = lax.rsqrt(total * (1.0 / D) + epsilon)
    inverse[...] = scale
    for j in range(NB):
        where = columns(place, j)
        value = (tok[:, where].astype(F32) * scale * gain[:, where].astype(F32)).astype(BF16)
        normed[j] = value
        if j >= 5:
            send[:, (7 - j) * B : (8 - j) * B] = value
    send[:, 3 * B : 4 * B] = cot[...]
    other = pl.multiple_of((1 - place[NB]) * H, H)
    send[:, 4 * B : 4 * B + H] = normed[4, :, pl.ds(other, H)]


def outer(a, b):
    return lax.dot_general(a, b, (((0,), (0,)), ((), ())), preferred_element_type=F32)


def grad_kernel(place, normed, cot, got, half, term3, term2, term1, own):
    mine = cot[...]
    theirs = got[:, 3 * B : 4 * B]
    here = pl.multiple_of(place[NB] * H, H)
    half[...] = (
        (outer(normed[4, :, pl.ds(here, H)], mine) + outer(got[:, 4 * B : 4 * B + H], theirs)) * SCALE
    ).astype(BF16)
    for j, term in ((3, term3), (2, term2), (1, term1)):
        term[...] = (
            outer(normed[j], mine) + outer(got[:, (j - 1) * B : j * B], theirs)
        ) * SCALE
    own[...] = outer(normed[0], mine) * SCALE


def token_kernel(
    place, tok, gain, inverse, normed, cot, w0, w7, w6, w5, h4, swapped, swapped4, keys, grad, w4, back
):
    here = pl.multiple_of(place[NB] * H, H)
    there = pl.multiple_of((1 - place[NB]) * H, H)
    w4[pl.ds(here, H), :] = h4[...]
    w4[pl.ds(there, H), :] = swapped4[...]
    blocks = (w0, swapped.at[0], swapped.at[1], swapped.at[2], w4, w5, w6, w7)
    mine = cot[...]
    total = jnp.zeros(keys.shape, F32)
    mixed = jnp.zeros((tok.shape[0], 1), F32)
    for j, block in enumerate(blocks):
        where = columns(place, j)
        w = block[...]
        total += jnp.dot(normed[j], w, preferred_element_type=F32)
        down = (
            lax.dot_general(mine, w, (((1,), (1,)), ((), ())), preferred_element_type=F32) * SCALE
        ).astype(BF16)
        back[j] = down
        up = down.astype(F32) * gain[:, where].astype(F32)
        mixed += jnp.sum(up * tok[:, where].astype(F32), axis=1, keepdims=True)
    keys[...] = (total * SCALE).astype(BF16)
    scale = inverse[...]
    factor = scale * scale * (mixed * (1.0 / D))
    for j in range(NB):
        where = columns(place, j)
        up = back[j].astype(F32) * gain[:, where].astype(F32)
        grad[:, where] = (scale * (up - tok[:, where].astype(F32) * factor)).astype(BF16)


def join_kernel(place, local, other_y, other_core, rows):
    core, y = place[NB], place[NB + 1]
    rows[2 * y + core] = local[0]
    rows[2 * (1 - y) + core] = other_y[0]
    rows[2 * y + 1 - core] = other_core[0]
    rows[2 * (1 - y) + 1 - core] = other_core[1]


def first_sum_kernel(place, term, got, earlier, total):
    here = pl.ds(pl.multiple_of(place[NB] * H, H), H)
    total[...] = term[...].astype(BF16)
    total[here, :] = (term[here, :] + got[...].astype(F32)).astype(BF16)


def sum_kernel(term, got, earlier, total):
    total[...] = (term[...] + got[...].astype(F32)).astype(BF16)


def core_kernel(place, own, got, keep, give):
    core = place[NB]
    for y in range(2):
        mine, theirs = 2 * y + core, 2 * y + 1 - core
        keep[y] = own[mine] + got[mine].astype(F32)
        give[y] = (own[theirs] + got[theirs].astype(F32)).astype(BF16)


def y_kernel(place, kept, got, keep, give):
    y = place[NB + 1]
    keep[...] = kept[y] + got[y].astype(F32)
    give[0] = (kept[1 - y] + got[1 - y].astype(F32)).astype(BF16)


def choose_kernel(matching, pieces, chosen):
    for d in range(pieces.shape[0]):
        chosen[d] = pieces[matching[d]]


def update_kernel(kept, got, weight, momentum, partner, new_weight, new_momentum):
    n = kept.shape[0]
    grad = (kept[...] + got[0].astype(F32)).astype(BF16).astype(F32)
    mean_weight = (weight[0].astype(F32) + partner[:n].astype(F32)) * 0.5
    mean_momentum = (momentum[0].astype(F32) + partner[n:].astype(F32)) * 0.5
    following = momentum_decay * mean_momentum + grad
    new_momentum[0] = following.astype(BF16)
    new_weight[0] = (mean_weight - outer_rate * (grad + momentum_decay * following)).astype(BF16)


def shape(dims, kind):
    return jax.ShapeDtypeStruct(dims, kind)


def call(kernel, name, out, specs, *args, scratch=(), vmem=12):
    single = not isinstance(out, tuple)
    return pl.pallas_call(
        kernel,
        out_shape=out,
        in_specs=specs,
        out_specs=VMEM if single else (VMEM,) * len(out),
        scratch_shapes=scratch,
        compiler_params=pltpu.CompilerParams(vmem_limit_bytes=vmem << 20),
        name=name,
    )(*args)


def per_device(tokens, norm_gain, weight, momentum, key_grad, matching):
    rows = tokens.shape[0]
    part = weight.shape[1]
    n = 32
    lane = jnp.arange(16, dtype=jnp.int32)
    me = jnp.full((16,), lax.axis_index("fsdp"), jnp.int32)
    group = jnp.full((16,), lax.axis_index("rep"), jnp.int32)
    core = me & 1
    place = jnp.where(lane < NB, ((me >> 2) + (2 * core - 1) * lane) & (NB - 1), group & 3)
    place = jnp.where(lane == NB, core, place)
    place = jnp.where(lane == NB + 1, (me >> 1) & 1, place)
    place = jnp.where(lane == NB + 2, group >> 2, place)
    gain = norm_gain[None]

    def along(v, perm):
        return lax.ppermute(v, "fsdp", perm)

    def after(v, *others):
        return lax.optimization_barrier((v, *others))

    swap_core = [(i, i ^ 1) for i in range(n)]
    swap_y = [(i, i ^ 2) for i in range(n)]
    on = [(i, (i + (4 if i % 2 else -4)) % n) for i in range(n)]

    def exchange(v):
        return lax.all_to_all(v, "rep", 0, 0)

    other_y = along(weight, swap_y)

    normed, send, inverse = call(
        norm_kernel,
        "norm",
        (shape((NB, rows, B), BF16), shape((rows, 4 * B + H), BF16), shape((rows, 1), F32)),
        [SMEM, VMEM, VMEM, VMEM],
        place,
        tokens,
        gain,
        key_grad,
    )
    both = jnp.concatenate([after(weight, inverse)[0][0], momentum[0]], axis=0)
    both = both.reshape(16, part // 8, K)
    send, other_y = after(send, other_y)
    got = along(send, swap_core)
    other_core = along(jnp.concatenate([weight, other_y], axis=0), swap_core)
    w0 = call(
        join_kernel,
        "join",
        shape((4, part, K), BF16),
        [SMEM, VMEM, VMEM, VMEM],
        place,
        weight,
        other_y,
        other_core,
    ).reshape(B, K)
    got = after(got, w0)[0]
    half, term3, term2, term1, own = call(
        grad_kernel,
        "weight_grad",
        (shape((H, K), BF16),) + (shape((B, K), F32),) * 4,
        [SMEM, VMEM, VMEM, VMEM],
        place,
        normed,
        key_grad,
        got,
    )

    block = shape((B, K), BF16)
    sums = [VMEM, VMEM, ANY]
    w7 = along(w0, on)
    s3 = along(half, on)
    w7 = after(w7, s3)[0]
    w6 = along(w7, on)
    p3 = call(first_sum_kernel, "sum_3", block, [SMEM] + sums, place, term3, s3, w7)
    s2 = along(p3, on)
    pieces = exchange(after(both, p3)[0])
    p2 = call(sum_kernel, "sum_2", block, sums, term2, s2, p3)
    w6 = after(w6, p2)[0]
    w5 = along(w6, on)
    s1 = along(p2, on)
    chosen = call(
        choose_kernel, "choose", shape(both.shape, BF16), [SMEM, VMEM], matching, pieces
    )
    p1 = call(sum_kernel, "sum_1", block, sums, term1, s1, chosen)
    w5 = after(w5, p1)[0]
    partner = exchange(after(chosen, p1)[0])
    core_here = lax.axis_index("fsdp") & 1
    h4 = along(lax.dynamic_slice_in_dim(w5, core_here * H, H, 0), on)
    partner = partner.reshape(2 * part, K)
    s0 = along(p1, on)
    swapped = along(jnp.stack([w7, w6, w5]), swap_core)
    swapped4 = along(h4, swap_core)

    kept, give = call(
        core_kernel,
        "core_sum",
        (shape((2, part, K), F32), shape((2, part, K), BF16)),
        [SMEM, VMEM, VMEM],
        place,
        own.reshape(4, part, K),
        s0.reshape(4, part, K),
    )
    got = along(give, swap_core)
    kept, give = call(
        y_kernel,
        "y_sum",
        (shape((part, K), F32), shape((1, part, K), BF16)),
        [SMEM, VMEM, VMEM],
        place,
        kept,
        got,
    )
    give, swapped4 = after(give, swapped4)
    got = along(give, swap_y)

    keys, token_grad = call(
        token_kernel,
        "token_grad",
        (shape((rows, K), BF16), shape((rows, D), BF16)),
        [SMEM] + [VMEM] * 12,
        place,
        tokens,
        gain,
        inverse,
        normed,
        key_grad,
        w0,
        w7,
        w6,
        w5,
        h4,
        swapped,
        swapped4,
        scratch=[pltpu.VMEM((B, K), BF16), pltpu.VMEM((NB, rows, B), BF16)],
        vmem=24,
    )
    keys, token_grad, got = after(keys, token_grad, got)
    new_weight, new_momentum = call(
        update_kernel,
        "update",
        (shape((1, part, K), BF16), shape((1, part, K), BF16)),
        [VMEM] * 5,
        kept,
        got,
        weight,
        momentum,
        partner,
        vmem=40,
    )
    return (keys, token_grad, new_weight, new_momentum)


def solution(mesh):
    in_specs = (
        P(("rep", "fsdp"), None),
        P(),
        P("rep", "fsdp", None),
        P("rep", "fsdp", None),
        P(("rep", "fsdp"), None),
        P(),
    )
    out_specs = (
        P(("rep", "fsdp"), None),
        P(("rep", "fsdp"), None),
        P("rep", "fsdp", None),
        P("rep", "fsdp", None),
    )
    return jax.shard_map(
        per_device, mesh=mesh, in_specs=in_specs, out_specs=out_specs, check_vma=False
    )
```

time: 162 us -> 127 us (0.78)
  the two profiles are of different devices: /device:TPU:43 before, /device:TPU:1 now
where the time goes in v2:
time: 127 us; the launch traced here: 126 us
  starting transfers between devices  55.3 us (44%)
  waiting for transfers between devices  24.6 us (19%)
  Pallas kernels  16.5 us (13%)
  blocking collectives  16.2 us (13%)
  local copies, waits for them, and re-layouts  11 us (9%)
  other arithmetic  1.4 us (1%)
    ppermute x15, starting transfers between devices, along(): return lax.ppermute(v, 'fsdp', perm)  51.1 us
    ppermute x15, waiting for transfers between devices, along(): return lax.ppermute(v, 'fsdp', perm)  24.6 us
    pallas_call x11, Pallas kernels, call(): pl.pallas_call(kernel, out_shape=out, in_specs=specs, out_specs=VMEM if s...  16.5 us
    all_to_all x1, blocking collectives, exchange(): return lax.all_to_all(v, 'rep', 0, 0)  16.2 us
    unnamed x42, local copies, waits for them, and re-layouts  9.56 us
    all_to_all x1, starting transfers between devices, exchange(): return lax.all_to_all(v, 'rep', 0, 0)  4.2 us
  transfers between devices with their start and end apart: 16, of which 7 were waited for; matrix products, arithmetic and copies ran while one was open for 1% of the time, Pallas kernels for 11%

profile of v2, /device:TPU:1, one launch (start us, length us, event | category | flops | bytes accessed | tf_op | source)
XLA Modules:
  0.0 126.0 jit_solution(13732963215892678422)
XLA Ops:
  0.6 8.3 %collective-permute-start = (bf16[1,128,512]{2,1,0:T(8,128)(2,1)}, bf16[1,128,512]{2,1,0:T(8,128)(2,1)S(1)}, u32[]{:S(2)}, u32[]{:S(2)}) collective-permute-start(bf16[1,128,512]{2,1,0:T(8,128)(2,1)} %weight.1), channel_id=1, source_target_pairs={{0,2},{1,3},{2,0},{3,1},{4,6},{5,7},{6,4},{7,5},{8,10},{9,11},{10,... | collective-permute-start | bytes 393224 | tf_op jit(solution)/shard_map/ppermute | solution.py:176
  8.9 0.7 broadcast_in_dim.17.gain
  9.7 1.5 %copy-done = bf16[240,4096]{1,0:T(8,128)(2,1)S(1)} copy-done((bf16[240,4096]{1,0:T(8,128)(2,1)S(1)}, bf16[240,4096]{1,0:T(8,128)(2,1)}, u32[]{:S(2)}) %copy-start) | copy-done | bytes 1966104
  11.2 0.9 copy-done.4
  12.2 1.5 %norm.1 = (bf16[8,240,512]{2,1,0:T(8,128)(2,1)S(1)}, bf16[240,2304]{1,0:T(8,128)(2,1)S(1)}, f32[240,1]{1,0:T(8,128)S(1)}) custom-call(s32[16]{0:T(128)S(1)} %compare_select_fusion.3.place, bf16[240,4096]{1,0:T(8,128)(2,1)S(1)} %copy-done, bf16[1,4096]{1,0:T(2,128)(2,1)S(1)} %broadcast_in_dim.17.gain, bf16[240,512]{1,0:T(8,128)(2,1)S(1)} %copy-done.4), custom_call_target="tpu_custom_call" | custom-call | tf_op jit(solution)/shard_map/norm/pallas_call | solution.py:150
  13.7 0.4 collective-permute-done.other_y
  14.1 7.4 %collective-permute-start.3 = (bf16[240,2304]{1,0:T(8,128)(2,1)S(1)}, bf16[240,2304]{1,0:T(8,128)(2,1)S(1)}, u32[]{:S(2)}, u32[]{:S(2)}) collective-permute-start(bf16[240,2304]{1,0:T(8,128)(2,1)S(1)} %get-tuple-element.38), channel_id=1, source_target_pairs={{0,1},{1,0},{2,3},{3,2},{4,5},{5,4},{6,7},{7,6},{8,9},{9,8},{10,11... | collective-permute-start | bytes 3317768 | tf_op jit(solution)/shard_map/ppermute | solution.py:176
  21.6 1.9 %collective-permute-start.1 = (bf16[2,128,512]{2,1,0:T(8,128)(2,1)S(1)}, bf16[2,128,512]{2,1,0:T(8,128)(2,1)S(1)}, u32[]{:S(2)}, u32[]{:S(2)}) collective-permute-start(bf16[2,128,512]{2,1,0:T(8,128)(2,1)S(1)} %pad_maximum_fusion.1), channel_id=1, source_target_pairs={{0,1},{1,0},{2,3},{3,2},{4,5},{5,4},{6,7},{7,6},{8,9},{9,8},{10,11... | collective-permute-start | bytes 786440 | tf_op jit(solution)/shard_map/ppermute | solution.py:176
  23.5 1.5 %collective-permute-done.1.other_core = bf16[2,128,512]{2,1,0:T(8,128)(2,1)S(1)} collective-permute-done((bf16[2,128,512]{2,1,0:T(8,128)(2,1)S(1)}, bf16[2,128,512]{2,1,0:T(8,128)(2,1)S(1)}, u32[]{:S(2)}, u32[]{:S(2)}) %collective-permute-start.1) | collective-permute-done | bytes 262176 | tf_op jit(solution)/shard_map/ppermute | solution.py:176
  25.0 0.6 join.1
  25.6 1.9 %collective-permute-start.2 = (bf16[512,512]{1,0:T(8,128)(2,1)S(1)}, bf16[512,512]{1,0:T(8,128)(2,1)S(1)}, u32[]{:S(2)}, u32[]{:S(2)}) collective-permute-start(bf16[512,512]{1,0:T(8,128)(2,1)S(1)} %bitcast.12), channel_id=1, source_target_pairs={{0,28},{1,5},{2,30},{3,7},{4,0},{5,9},{6,2},{7,11},{8,4},{9,13},{1... | collective-permute-start | bytes 1572872 | tf_op jit(solution)/shard_map/ppermute | solution.py:176
  27.6 1.8 %weight_grad.1 = (bf16[256,512]{1,0:T(8,128)(2,1)S(1)}, f32[512,512]{1,0:T(8,128)S(1)}, f32[512,512]{1,0:T(8,128)S(1)}, f32[512,512]{1,0:T(8,128)S(1)}, f32[512,512]{1,0:T(8,128)S(1)}) custom-call(s32[16]{0:T(128)S(1)} %compare_select_fusion.3.place, bf16[8,240,512]{2,1,0:T(8,128)(2,1)S(1)} %get-tuple-element.35.normed, bf16[240,512]{1,0:T(8,128)(2,1)S(1)} %copy-done.5, ...), custom_call_target="tpu_custom_call" | custom-call | tf_op jit(solution)/shard_map/weight_grad/pallas_call | solution.py:150
  29.4 1.9 %collective-permute-start.4 = (bf16[256,512]{1,0:T(8,128)(2,1)S(1)}, bf16[256,512]{1,0:T(8,128)(2,1)S(1)}, u32[]{:S(2)}, u32[]{:S(2)}) collective-permute-start(bf16[256,512]{1,0:T(8,128)(2,1)S(1)} %get-tuple-element.40), channel_id=1, source_target_pairs={{0,28},{1,5},{2,30},{3,7},{4,0},{5,9},{6,2},{7,11},{8,4},{9,13},{1... | collective-permute-start | bytes 786440 | tf_op jit(solution)/shard_map/ppermute | solution.py:176
  31.4 6.5 %collective-permute-done.2.earlier.w7 = bf16[512,512]{1,0:T(8,128)(2,1)S(1)} collective-permute-done((bf16[512,512]{1,0:T(8,128)(2,1)S(1)}, bf16[512,512]{1,0:T(8,128)(2,1)S(1)}, u32[]{:S(2)}, u32[]{:S(2)}) %collective-permute-start.2) | collective-permute-done | bytes 524320 | tf_op jit(solution)/shard_map/ppermute | solution.py:176
  37.9 2.8 %collective-permute-done.4.got = bf16[256,512]{1,0:T(8,128)(2,1)S(1)} collective-permute-done((bf16[256,512]{1,0:T(8,128)(2,1)S(1)}, bf16[256,512]{1,0:T(8,128)(2,1)S(1)}, u32[]{:S(2)}, u32[]{:S(2)}) %collective-permute-start.4) | collective-permute-done | bytes 262176 | tf_op jit(solution)/shard_map/ppermute | solution.py:176
  40.7 0.6 sum_3.1.earlier
  41.4 2.1 %collective-permute-start.6 = (bf16[512,512]{1,0:T(8,128)(2,1)S(1)}, bf16[512,512]{1,0:T(8,128)(2,1)S(1)}, u32[]{:S(2)}, u32[]{:S(2)}) collective-permute-start(bf16[512,512]{1,0:T(8,128)(2,1)S(1)} %sum_3.1.earlier), channel_id=1, source_target_pairs={{0,28},{1,5},{2,30},{3,7},{4,0},{5,9},{6,2},{7,11},{8,4},{9,13},{1... | collective-permute-start | bytes 1572872 | tf_op jit(solution)/shard_map/ppermute | solution.py:176
  43.4 1.9 %collective-permute-start.5 = (bf16[512,512]{1,0:T(8,128)(2,1)S(1)}, bf16[512,512]{1,0:T(8,128)(2,1)S(1)}, u32[]{:S(2)}, u32[]{:S(2)}) collective-permute-start(bf16[512,512]{1,0:T(8,128)(2,1)S(1)} %collective-permute-done.2.earlier.w7), channel_id=1, source_target_pairs={{0,28},{1,5},{2,30},{3,7},{4,0},{5,9},{6,2},{7,11},{8,4},{9,13},{1... | collective-permute-start | bytes 1572872 | tf_op jit(solution)/shard_map/ppermute | solution.py:176
  45.3 7.3 %collective-permute-done.6.got = bf16[512,512]{1,0:T(8,128)(2,1)S(1)} collective-permute-done((bf16[512,512]{1,0:T(8,128)(2,1)S(1)}, bf16[512,512]{1,0:T(8,128)(2,1)S(1)}, u32[]{:S(2)}, u32[]{:S(2)}) %collective-permute-start.6) | collective-permute-done | bytes 524320 | tf_op jit(solution)/shard_map/ppermute | solution.py:176
  52.6 0.1 sum_2.1
  52.8 1.9 %collective-permute-start.8 = (bf16[512,512]{1,0:T(8,128)(2,1)S(1)}, bf16[512,512]{1,0:T(8,128)(2,1)S(1)}, u32[]{:S(2)}, u32[]{:S(2)}) collective-permute-start(bf16[512,512]{1,0:T(8,128)(2,1)S(1)} %sum_2.1), channel_id=1, source_target_pairs={{0,28},{1,5},{2,30},{3,7},{4,0},{5,9},{6,2},{7,11},{8,4},{9,13},{1... | collective-permute-start | bytes 1572872 | tf_op jit(solution)/shard_map/ppermute | solution.py:176
  54.7 3.5 %collective-permute-done.5.w6 = bf16[512,512]{1,0:T(8,128)(2,1)S(1)} collective-permute-done((bf16[512,512]{1,0:T(8,128)(2,1)S(1)}, bf16[512,512]{1,0:T(8,128)(2,1)S(1)}, u32[]{:S(2)}, u32[]{:S(2)}) %collective-permute-start.5) | collective-permute-done | bytes 524320 | tf_op jit(solution)/shard_map/ppermute | solution.py:176
  58.2 1.9 %collective-permute-start.7 = (bf16[512,512]{1,0:T(8,128)(2,1)S(1)}, bf16[512,512]{1,0:T(8,128)(2,1)S(1)}, u32[]{:S(2)}, u32[]{:S(2)}) collective-permute-start(bf16[512,512]{1,0:T(8,128)(2,1)S(1)} %collective-permute-done.5.w6), channel_id=1, source_target_pairs={{0,28},{1,5},{2,30},{3,7},{4,0},{5,9},{6,2},{7,11},{8,4},{9,13},{1... | collective-permute-start | bytes 1572872 | tf_op jit(solution)/shard_map/ppermute | solution.py:176
  60.2 16.2 %all_to_all.10.pieces = bf16[16,16,512]{2,1,0:T(8,128)(2,1)S(1)} all-to-all(bf16[16,16,512]{2,1,0:T(8,128)(2,1)S(1)} %bitcast.18), channel_id=1, replica_groups=mesh['rep'=16,'fsdp'=32] {'rep'}, dimensions={0} | all-to-all | bytes 524288 | tf_op jit(solution)/shard_map/all_to_all | solution.py:186
  76.4 1.3 %choose.1.earlier = bf16[16,16,512]{2,1,0:T(8,128)(2,1)} custom-call(s32[16]{0:T(128)S(1)} %copy-done.20, bf16[16,16,512]{2,1,0:T(8,128)(2,1)S(1)} %all_to_all.10.pieces), custom_call_target="tpu_custom_call" | custom-call | tf_op jit(solution)/shard_map/choose/pallas_call | solution.py:150
  77.6 0.9 sum_1.1
  78.5 1.3 %pad_maximum_fusion = bf16[3,512,512]{2,1,0:T(8,128)(2,1)} fusion(bf16[1,512,512]{2,1,0:T(8,128)(2,1)S(1)} %bitcast.11, bf16[1,512,512]{2,1,0:T(8,128)(2,1)S(1)} %bitcast.14, bf16[1,512,512]{2,1,0:T(8,128)(2,1)S(1)} %bitcast.10), kind=kLoop, calls=%fused_computation | loop fusion | flops 1572864 | bytes 3145728 | tf_op jit(solution)/shard_map/stack | solution.py:250
  79.9 8.7 %collective-permute-start.10 = (bf16[3,512,512]{2,1,0:T(8,128)(2,1)}, bf16[3,512,512]{2,1,0:T(8,128)(2,1)}, u32[]{:S(2)}, u32[]{:S(2)}) collective-permute-start(bf16[3,512,512]{2,1,0:T(8,128)(2,1)} %pad_maximum_fusion), channel_id=1, source_target_pairs={{0,1},{1,0},{2,3},{3,2},{4,5},{5,4},{6,7},{7,6},{8,9},{9,8},{10,11... | collective-permute-start | bytes 4718600 | tf_op jit(solution)/shard_map/ppermute | solution.py:176
  88.6 1.9 %collective-permute-start.11 = (bf16[512,512]{1,0:T(8,128)(2,1)}, bf16[512,512]{1,0:T(8,128)(2,1)}, u32[]{:S(2)}, u32[]{:S(2)}) collective-permute-start(bf16[512,512]{1,0:T(8,128)(2,1)} %sum_1.1), channel_id=1, source_target_pairs={{0,28},{1,5},{2,30},{3,7},{4,0},{5,9},{6,2},{7,11},{8,4},{9,13},{1... | collective-permute-start | bytes 1572872 | tf_op jit(solution)/shard_map/ppermute | solution.py:176
  90.5 0.7 constant_dynamic-slice_fusion
  91.2 2.0 %collective-permute-start.9 = (bf16[256,512]{1,0:T(8,128)(2,1)}, bf16[256,512]{1,0:T(8,128)(2,1)}, u32[]{:S(2)}, u32[]{:S(2)}) collective-permute-start(bf16[256,512]{1,0:T(8,128)(2,1)} %constant_dynamic-slice_fusion), channel_id=1, source_target_pairs={{0,28},{1,5},{2,30},{3,7},{4,0},{5,9},{6,2},{7,11},{8,4},{9,13},{1... | collective-permute-start | bytes 786440 | tf_op jit(solution)/shard_map/ppermute | solution.py:176
  93.3 4.2 %all-to-all-start.1 = ((bf16[16,16,512]{2,1,0:T(8,128)(2,1)}), bf16[16,16,512]{2,1,0:T(8,128)(2,1)}, u32[]{:S(2)}, u32[]{:S(2)}) async-start(bf16[16,16,512]{2,1,0:T(8,128)(2,1)} %choose.1.earlier), calls=%async_computation.1 | async-start | bytes 524288 | tf_op jit(solution)/shard_map/all_to_all | solution.py:186
  97.5 2.5 %collective-permute-done.11 = bf16[512,512]{1,0:T(8,128)(2,1)} collective-permute-done((bf16[512,512]{1,0:T(8,128)(2,1)}, bf16[512,512]{1,0:T(8,128)(2,1)}, u32[]{:S(2)}, u32[]{:S(2)}) %collective-permute-start.11) | collective-permute-done | bytes 524320 | tf_op jit(solution)/shard_map/ppermute | solution.py:176
  100.0 1.2 copy-done.12
  101.2 1.2 core_sum.1
  102.4 1.9 %collective-permute-start.12 = (bf16[2,128,512]{2,1,0:T(8,128)(2,1)S(1)}, bf16[2,128,512]{2,1,0:T(8,128)(2,1)S(1)}, u32[]{:S(2)}, u32[]{:S(2)}) collective-permute-start(bf16[2,128,512]{2,1,0:T(8,128)(2,1)S(1)} %get-tuple-element.51), channel_id=1, source_target_pairs={{0,1},{1,0},{2,3},{3,2},{4,5},{5,4},{6,7},{7,6},{8,9},{9,8},{10,11... | collective-permute-start | bytes 786440 | tf_op jit(solution)/shard_map/ppermute | solution.py:176
  104.4 2.4 %collective-permute-start.13 = (bf16[256,512]{1,0:T(8,128)(2,1)}, bf16[256,512]{1,0:T(8,128)(2,1)S(1)}, u32[]{:S(2)}, u32[]{:S(2)}) collective-permute-start(bf16[256,512]{1,0:T(8,128)(2,1)} %collective-permute-done.9.h4), channel_id=1, source_target_pairs={{0,1},{1,0},{2,3},{3,2},{4,5},{5,4},{6,7},{7,6},{8,9},{9,8},{10,11... | collective-permute-start | bytes 786440 | tf_op jit(solution)/shard_map/ppermute | solution.py:176
  106.8 0.6 y_sum.1
  107.4 0.7 copy-done.14
  108.1 0.0 collective-permute-done.13.swapped4
  108.2 4.8 %collective-permute-start.14 = (bf16[1,128,512]{2,1,0:T(8,128)(2,1)S(1)}, bf16[1,128,512]{2,1,0:T(8,128)(2,1)S(1)}, u32[]{:S(2)}, u32[]{:S(2)}) collective-permute-start(bf16[1,128,512]{2,1,0:T(8,128)(2,1)S(1)} %get-tuple-element.56), channel_id=1, source_target_pairs={{0,2},{1,3},{2,0},{3,1},{4,6},{5,7},{6,4},{7,5},{8,10},{9,11},{10,... | collective-permute-start | bytes 393224 | tf_op jit(solution)/shard_map/ppermute | solution.py:176
  113.0 1.5 %copy-done.3 = bf16[8,240,512]{2,1,0:T(8,128)(2,1)S(1)} copy-done((bf16[8,240,512]{2,1,0:T(8,128)(2,1)S(1)}, bf16[8,240,512]{2,1,0:T(8,128)(2,1)}, u32[]{:S(2)}) %copy-start.3) | copy-done | bytes 1966104
  114.6 1.0 copy-done.9
  115.6 6.1 %token_grad.1 = (bf16[240,512]{1,0:T(8,128)(2,1)}, bf16[240,4096]{1,0:T(8,128)(2,1)}) custom-call(s32[16]{0:T(128)S(1)} %compare_select_fusion.3.place, bf16[240,4096]{1,0:T(8,128)(2,1)S(1)} %copy-done.1, bf16[1,4096]{1,0:T(2,128)(2,1)S(1)} %broadcast_in_dim.17.gain, f32[240,1]{1,0:T(8,128)S(1)} %copy-done.19, bf16[8,240,512]{2,1,0:T(8,128)(2,1)S(1)} %copy-done.3, ...), custom_call_target="tpu_custom_call" | custom-call | tf_op jit(solution)/shard_map/token_grad/pallas_call | solution.py:150
  121.7 0.7 copy-done.16
  122.4 0.9 copy-done.15
  123.4 0.9 copy-done.17
  124.3 1.8 %update.1 = (bf16[1,128,512]{2,1,0:T(8,128)(2,1)}, bf16[1,128,512]{2,1,0:T(8,128)(2,1)}) custom-call(f32[128,512]{1,0:T(8,128)S(1)} %copy-done.15, bf16[1,128,512]{2,1,0:T(8,128)(2,1)S(1)} %copy-done.17, bf16[1,128,512]{2,1,0:T(8,128)(2,1)S(1)} %copy-done.10, bf16[1,128,512]{2,1,0:T(8,128)(2,1)S(1)} %copy-done.13, bf16[256,512]{1,0:T(8,128)(2,1)} %bitcast.9.partner), custom_call_target="tpu_custom_call" | custom-call | tf_op jit(solution)/shard_map/update/pallas_call | solution.py:150
  (44 shorter events, 0.2 us)
Async XLA Ops:
  0.6 13.5 %collective-permute-start = (bf16[1,128,512]{2,1,0:T(8,128)(2,1)}, bf16[1,128,512]{2,1,0:T(8,128)(2,1)S(1)}, u32[]{:S(2)}, u32[]{:S(2)}) collective-permute-start(bf16[1,128,512]{2,1,0:T(8,128)(2,1)} %weight.1), channel_id=1, source_target_pairs={{0,2},{1,3},{2,0},{3,1},{4,6},{5,7},{6,4},{7,5},{8,10},{9,11},{10,... | collective-permute-start | bytes 393224 | tf_op jit(solution)/shard_map/ppermute | solution.py:176
  9.7 1.5 %copy-start = (bf16[240,4096]{1,0:T(8,128)(2,1)S(1)}, bf16[240,4096]{1,0:T(8,128)(2,1)}, u32[]{:S(2)}) copy-start(bf16[240,4096]{1,0:T(8,128)(2,1)} %tok.3) | copy-start | bytes 5898244
  11.2 0.9 copy-start.4
  12.2 9.4 %copy-start.10 = (bf16[1,128,512]{2,1,0:T(8,128)(2,1)S(1)}, bf16[1,128,512]{2,1,0:T(8,128)(2,1)}, u32[]{:S(2)}) copy-start(bf16[1,128,512]{2,1,0:T(8,128)(2,1)} %weight.1) | copy-start | bytes 393220
  12.2 15.4 %copy-start.5 = (bf16[240,512]{1,0:T(8,128)(2,1)S(1)}, bf16[240,512]{1,0:T(8,128)(2,1)}, u32[]{:S(2)}) copy-start(bf16[240,512]{1,0:T(8,128)(2,1)} %cot.5) | copy-start | bytes 737284
  13.7 15.7 %copy-start.2 = (bf16[8,240,512]{2,1,0:T(8,128)(2,1)}, bf16[8,240,512]{2,1,0:T(8,128)(2,1)S(1)}, u32[]{:S(2)}) copy-start(bf16[8,240,512]{2,1,0:T(8,128)(2,1)S(1)} %get-tuple-element.35.normed) | copy-start | bytes 5898244
  13.7 15.7 %copy-start.18 = (f32[240,1]{1,0:T(8,128)}, f32[240,1]{1,0:T(8,128)S(1)}, u32[]{:S(2)}) copy-start(f32[240,1]{1,0:T(8,128)S(1)} %get-tuple-element.34.inverse) | copy-start | bytes 2884
  14.1 13.4 %collective-permute-start.3 = (bf16[240,2304]{1,0:T(8,128)(2,1)S(1)}, bf16[240,2304]{1,0:T(8,128)(2,1)S(1)}, u32[]{:S(2)}, u32[]{:S(2)}) collective-permute-start(bf16[240,2304]{1,0:T(8,128)(2,1)S(1)} %get-tuple-element.38), channel_id=1, source_target_pairs={{0,1},{1,0},{2,3},{3,2},{4,5},{5,4},{6,7},{7,6},{8,9},{9,8},{10,11... | collective-permute-start | bytes 3317768 | tf_op jit(solution)/shard_map/ppermute | solution.py:176
  21.6 3.4 %collective-permute-start.1 = (bf16[2,128,512]{2,1,0:T(8,128)(2,1)S(1)}, bf16[2,128,512]{2,1,0:T(8,128)(2,1)S(1)}, u32[]{:S(2)}, u32[]{:S(2)}) collective-permute-start(bf16[2,128,512]{2,1,0:T(8,128)(2,1)S(1)} %pad_maximum_fusion.1), channel_id=1, source_target_pairs={{0,1},{1,0},{2,3},{3,2},{4,5},{5,4},{6,7},{7,6},{8,9},{9,8},{10,11... | collective-permute-start | bytes 786440 | tf_op jit(solution)/shard_map/ppermute | solution.py:176
  25.6 3.8 %copy-start.6 = (bf16[4,128,512]{2,1,0:T(8,128)(2,1)}, bf16[4,128,512]{2,1,0:T(8,128)(2,1)S(1)}, u32[]{:S(2)}) copy-start(bf16[4,128,512]{2,1,0:T(8,128)(2,1)S(1)} %join.1) | copy-start | bytes 1572868
  25.6 12.3 %collective-permute-start.2 = (bf16[512,512]{1,0:T(8,128)(2,1)S(1)}, bf16[512,512]{1,0:T(8,128)(2,1)S(1)}, u32[]{:S(2)}, u32[]{:S(2)}) collective-permute-start(bf16[512,512]{1,0:T(8,128)(2,1)S(1)} %bitcast.12), channel_id=1, source_target_pairs={{0,28},{1,5},{2,30},{3,7},{4,0},{5,9},{6,2},{7,11},{8,4},{9,13},{1... | collective-permute-start | bytes 1572872 | tf_op jit(solution)/shard_map/ppermute | solution.py:176
  29.4 11.9 %copy-start.11 = (f32[512,512]{1,0:T(8,128)}, f32[512,512]{1,0:T(8,128)S(1)}, u32[]{:S(2)}) copy-start(f32[512,512]{1,0:T(8,128)S(1)} %get-tuple-element.49) | copy-start | bytes 3145732
  29.4 11.2 %collective-permute-start.4 = (bf16[256,512]{1,0:T(8,128)(2,1)S(1)}, bf16[256,512]{1,0:T(8,128)(2,1)S(1)}, u32[]{:S(2)}, u32[]{:S(2)}) collective-permute-start(bf16[256,512]{1,0:T(8,128)(2,1)S(1)} %get-tuple-element.40), channel_id=1, source_target_pairs={{0,28},{1,5},{2,30},{3,7},{4,0},{5,9},{6,2},{7,11},{8,4},{9,13},{1... | collective-permute-start | bytes 786440 | tf_op jit(solution)/shard_map/ppermute | solution.py:176
  41.3 18.8 %copy-start.13 = (bf16[1,128,512]{2,1,0:T(8,128)(2,1)S(1)}, bf16[1,128,512]{2,1,0:T(8,128)(2,1)}, u32[]{:S(2)}) copy-start(bf16[1,128,512]{2,1,0:T(8,128)(2,1)} %momentum.1) | copy-start | bytes 393220
  41.4 11.3 %collective-permute-start.6 = (bf16[512,512]{1,0:T(8,128)(2,1)S(1)}, bf16[512,512]{1,0:T(8,128)(2,1)S(1)}, u32[]{:S(2)}, u32[]{:S(2)}) collective-permute-start(bf16[512,512]{1,0:T(8,128)(2,1)S(1)} %sum_3.1.earlier), channel_id=1, source_target_pairs={{0,28},{1,5},{2,30},{3,7},{4,0},{5,9},{6,2},{7,11},{8,4},{9,13},{1... | collective-permute-start | bytes 1572872 | tf_op jit(solution)/shard_map/ppermute | solution.py:176
  43.4 14.8 %collective-permute-start.5 = (bf16[512,512]{1,0:T(8,128)(2,1)S(1)}, bf16[512,512]{1,0:T(8,128)(2,1)S(1)}, u32[]{:S(2)}, u32[]{:S(2)}) collective-permute-start(bf16[512,512]{1,0:T(8,128)(2,1)S(1)} %collective-permute-done.2.earlier.w7), channel_id=1, source_target_pairs={{0,28},{1,5},{2,30},{3,7},{4,0},{5,9},{6,2},{7,11},{8,4},{9,13},{1... | collective-permute-start | bytes 1572872 | tf_op jit(solution)/shard_map/ppermute | solution.py:176
  52.6 23.8 %copy-start.20 = (s32[16]{0:T(128)S(1)}, s32[16]{0:T(128)}, u32[]{:S(2)}) copy-start(s32[16]{0:T(128)} %matching.1) | copy-start | bytes 196
  52.8 24.9 %collective-permute-start.8 = (bf16[512,512]{1,0:T(8,128)(2,1)S(1)}, bf16[512,512]{1,0:T(8,128)(2,1)S(1)}, u32[]{:S(2)}, u32[]{:S(2)}) collective-permute-start(bf16[512,512]{1,0:T(8,128)(2,1)S(1)} %sum_2.1), channel_id=1, source_target_pairs={{0,28},{1,5},{2,30},{3,7},{4,0},{5,9},{6,2},{7,11},{8,4},{9,13},{1... | collective-permute-start | bytes 1572872 | tf_op jit(solution)/shard_map/ppermute | solution.py:176
  58.2 20.3 %copy-start.8 = (bf16[512,512]{1,0:T(8,128)(2,1)}, bf16[512,512]{1,0:T(8,128)(2,1)S(1)}, u32[]{:S(2)}) copy-start(bf16[512,512]{1,0:T(8,128)(2,1)S(1)} %collective-permute-done.5.w6) | copy-start | bytes 1572868
  58.2 20.3 %collective-permute-start.7 = (bf16[512,512]{1,0:T(8,128)(2,1)S(1)}, bf16[512,512]{1,0:T(8,128)(2,1)S(1)}, u32[]{:S(2)}, u32[]{:S(2)}) collective-permute-start(bf16[512,512]{1,0:T(8,128)(2,1)S(1)} %collective-permute-done.5.w6), channel_id=1, source_target_pairs={{0,28},{1,5},{2,30},{3,7},{4,0},{5,9},{6,2},{7,11},{8,4},{9,13},{1... | collective-permute-start | bytes 1572872 | tf_op jit(solution)/shard_map/ppermute | solution.py:176
  79.9 33.1 %collective-permute-start.10 = (bf16[3,512,512]{2,1,0:T(8,128)(2,1)}, bf16[3,512,512]{2,1,0:T(8,128)(2,1)}, u32[]{:S(2)}, u32[]{:S(2)}) collective-permute-start(bf16[3,512,512]{2,1,0:T(8,128)(2,1)} %pad_maximum_fusion), channel_id=1, source_target_pairs={{0,1},{1,0},{2,3},{3,2},{4,5},{5,4},{6,7},{7,6},{8,9},{9,8},{10,11... | collective-permute-start | bytes 4718600 | tf_op jit(solution)/shard_map/ppermute | solution.py:176
  88.6 11.5 %collective-permute-start.11 = (bf16[512,512]{1,0:T(8,128)(2,1)}, bf16[512,512]{1,0:T(8,128)(2,1)}, u32[]{:S(2)}, u32[]{:S(2)}) collective-permute-start(bf16[512,512]{1,0:T(8,128)(2,1)} %sum_1.1), channel_id=1, source_target_pairs={{0,28},{1,5},{2,30},{3,7},{4,0},{5,9},{6,2},{7,11},{8,4},{9,13},{1... | collective-permute-start | bytes 1572872 | tf_op jit(solution)/shard_map/ppermute | solution.py:176
  91.2 21.8 %copy-start.1 = (bf16[240,4096]{1,0:T(8,128)(2,1)S(1)}, bf16[240,4096]{1,0:T(8,128)(2,1)}, u32[]{:S(2)}) copy-start(bf16[240,4096]{1,0:T(8,128)(2,1)} %tok.3) | copy-start | bytes 5898244
  91.2 13.2 %collective-permute-start.9 = (bf16[256,512]{1,0:T(8,128)(2,1)}, bf16[256,512]{1,0:T(8,128)(2,1)}, u32[]{:S(2)}, u32[]{:S(2)}) collective-permute-start(bf16[256,512]{1,0:T(8,128)(2,1)} %constant_dynamic-slice_fusion), channel_id=1, source_target_pairs={{0,28},{1,5},{2,30},{3,7},{4,0},{5,9},{6,2},{7,11},{8,4},{9,13},{1... | collective-permute-start | bytes 786440 | tf_op jit(solution)/shard_map/ppermute | solution.py:176
  93.3 29.1 %all-to-all-start.1 = ((bf16[16,16,512]{2,1,0:T(8,128)(2,1)}), bf16[16,16,512]{2,1,0:T(8,128)(2,1)}, u32[]{:S(2)}, u32[]{:S(2)}) async-start(bf16[16,16,512]{2,1,0:T(8,128)(2,1)} %choose.1.earlier), calls=%async_computation.1 | async-start | bytes 524288 | tf_op jit(solution)/shard_map/all_to_all | solution.py:186
  97.5 15.5 %copy-start.7 = (bf16[4,128,512]{2,1,0:T(8,128)(2,1)S(1)}, bf16[4,128,512]{2,1,0:T(8,128)(2,1)}, u32[]{:S(2)}) copy-start(bf16[4,128,512]{2,1,0:T(8,128)(2,1)} %copy-done.6) | copy-start | bytes 1572868
  100.0 1.2 copy-start.12
  101.2 11.8 %copy-start.19 = (f32[240,1]{1,0:T(8,128)S(1)}, f32[240,1]{1,0:T(8,128)}, u32[]{:S(2)}) copy-start(f32[240,1]{1,0:T(8,128)} %copy-done.18) | copy-start | bytes 2884
  102.4 4.4 %collective-permute-start.12 = (bf16[2,128,512]{2,1,0:T(8,128)(2,1)S(1)}, bf16[2,128,512]{2,1,0:T(8,128)(2,1)S(1)}, u32[]{:S(2)}, u32[]{:S(2)}) collective-permute-start(bf16[2,128,512]{2,1,0:T(8,128)(2,1)S(1)} %get-tuple-element.51), channel_id=1, source_target_pairs={{0,1},{1,0},{2,3},{3,2},{4,5},{5,4},{6,7},{7,6},{8,9},{9,8},{10,11... | collective-permute-start | bytes 786440 | tf_op jit(solution)/shard_map/ppermute | solution.py:176
  104.4 3.8 %collective-permute-start.13 = (bf16[256,512]{1,0:T(8,128)(2,1)}, bf16[256,512]{1,0:T(8,128)(2,1)S(1)}, u32[]{:S(2)}, u32[]{:S(2)}) collective-permute-start(bf16[256,512]{1,0:T(8,128)(2,1)} %collective-permute-done.9.h4), channel_id=1, source_target_pairs={{0,1},{1,0},{2,3},{3,2},{4,5},{5,4},{6,7},{7,6},{8,9},{9,8},{10,11... | collective-permute-start | bytes 786440 | tf_op jit(solution)/shard_map/ppermute | solution.py:176
  107.4 0.7 copy-start.14
  108.2 13.6 %collective-permute-start.14 = (bf16[1,128,512]{2,1,0:T(8,128)(2,1)S(1)}, bf16[1,128,512]{2,1,0:T(8,128)(2,1)S(1)}, u32[]{:S(2)}, u32[]{:S(2)}) collective-permute-start(bf16[1,128,512]{2,1,0:T(8,128)(2,1)S(1)} %get-tuple-element.56), channel_id=1, source_target_pairs={{0,2},{1,3},{2,0},{3,1},{4,6},{5,7},{6,4},{7,5},{8,10},{9,11},{10,... | collective-permute-start | bytes 393224 | tf_op jit(solution)/shard_map/ppermute | solution.py:176
  113.0 1.5 %copy-start.3 = (bf16[8,240,512]{2,1,0:T(8,128)(2,1)S(1)}, bf16[8,240,512]{2,1,0:T(8,128)(2,1)}, u32[]{:S(2)}) copy-start(bf16[8,240,512]{2,1,0:T(8,128)(2,1)} %copy-done.2) | copy-start | bytes 5898244
  114.6 1.0 copy-start.9
  121.7 0.7 copy-start.16
  122.4 1.0 copy-start.15
  123.4 0.9 copy-start.17

commit v3 on v2

--- a/solution.py
+++ b/solution.py
@@ -28,20 +28,37 @@
     return pl.ds(pl.multiple_of(place[slot] * B, B), B)
 
 
-def norm_kernel(place, tok, gain, cot, normed, send, inverse):
-    total = jnp.zeros((tok.shape[0], 1), F32)
-    for j in range(NB):
-        part = tok[:, j * B : (j + 1) * B].astype(F32)
-        total += jnp.sum(part * part, axis=1, keepdims=True)
-    scale = lax.rsqrt(total * (1.0 / D) + epsilon)
-    inverse[...] = scale
-    for j in range(NB):
-        where = columns(place, j)
-        value = (tok[:, where].astype(F32) * scale * gain[:, where].astype(F32)).astype(BF16)
-        normed[j] = value
-        if j >= 5:
-            send[:, (7 - j) * B : (8 - j) * B] = value
-    send[:, 3 * B : 4 * B] = cot[...]
+def norm_kernel(place, tok_in, gain, cot, normed, send, inverse, tok, sems):
+    count = tok.shape[0]
+    chunk = 80 if count % 80 == 0 else count
+    starts = range(0, count, chunk)
+    loads = [
+        pltpu.make_async_copy(
+            tok_in.at[pl.ds(a, chunk)], tok.at[pl.ds(a, chunk)], sems.at[a // chunk]
+        )
+        for a in starts
+    ]
+    loads.append(pltpu.make_async_copy(cot, send.at[:, pl.ds(3 * B, B)], sems.at[len(starts)]))
+    for load in loads:
+        load.start()
+    for a, load in zip(starts, loads):
+        load.wait()
+        rows = slice(a, a + chunk)
+        total = jnp.zeros((chunk, 1), F32)
+        for j in range(NB):
+            part = tok[rows, j * B : (j + 1) * B].astype(F32)
+            total += jnp.sum(part * part, axis=1, keepdims=True)
+        scale = lax.rsqrt(total * (1.0 / D) + epsilon)
+        inverse[rows, :] = scale
+        for j in range(NB):
+            where = columns(place, j)
+            value = (tok[rows, where].astype(F32) * scale * gain[:, where].astype(F32)).astype(
+                BF16
+            )
+            normed[j, rows, :] = value
+            if j >= 5:
+                send[rows, (7 - j) * B : (8 - j) * B] = value
+    loads[-1].wait()
     other = pl.multiple_of((1 - place[NB]) * H, H)
     send[:, 4 * B : 4 * B + H] = normed[4, :, pl.ds(other, H)]
 
@@ -191,11 +208,13 @@
         norm_kernel,
         "norm",
         (shape((NB, rows, B), BF16), shape((rows, 4 * B + H), BF16), shape((rows, 1), F32)),
-        [SMEM, VMEM, VMEM, VMEM],
+        [SMEM, ANY, VMEM, ANY],
         place,
         tokens,
         gain,
         key_grad,
+        scratch=[pltpu.VMEM((rows, D), BF16), pltpu.SemaphoreType.DMA((4,))],
+        vmem=56,
     )
     both = jnp.concatenate([after(weight, inverse)[0][0], momentum[0]], axis=0)
     both = both.reshape(16, part // 8, K)
@@ -291,7 +310,7 @@
         swapped,
         swapped4,
         scratch=[pltpu.VMEM((B, K), BF16), pltpu.VMEM((NB, rows, B), BF16)],
-        vmem=24,
+        vmem=56,
     )
     keys, token_grad, got = after(keys, token_grad, got)
     new_weight, new_momentum = call(

time: 127 us -> 121 us (0.953)
  local copies, waits for them, and re-layouts: 11 us -> 3.63 us
  Pallas kernels: 16.5 us -> 19.3 us
  blocking collectives: 16.2 us -> 14.4 us
  waiting for transfers between devices: 24.6 us -> 26 us
    unnamed x42 -> x24, local copies, waits for them, and re-layouts: 9.56 us -> 1.58 us
    pallas_call x11, Pallas kernels: 16.5 us -> 19.3 us  [call(): pl.pallas_call(kernel, out_shape=out, in_specs=specs, out_specs=VMEM if s...]
    all_to_all x1, blocking collectives: 16.2 us -> 14.4 us  [exchange(): return lax.all_to_all(v, 'rep', 0, 0)]
    ppermute x15, waiting for transfers between devices: 24.6 us -> 26 us  [along(): return lax.ppermute(v, 'fsdp', perm)]
  transfers between devices with their start and end apart: 16 -> 16, of which waited for: 7 -> 9; matrix products, arithmetic and copies ran while one was open for 1% -> 2% of each run, Pallas kernels for 11% -> 15%
where the time goes in v3:
time: 121 us; the launch traced here: 120 us
  starting transfers between devices  54.1 us (45%)
  waiting for transfers between devices  26 us (21%)
  Pallas kernels  19.3 us (16%)
  blocking collectives  14.4 us (12%)
  local copies, waits for them, and re-layouts  3.63 us (3%)
  other arithmetic  1.94 us (2%)
    ppermute x15, starting transfers between devices, along(): return lax.ppermute(v, 'fsdp', perm)  50.5 us
    ppermute x15, waiting for transfers between devices, along(): return lax.ppermute(v, 'fsdp', perm)  26 us
    pallas_call x11, Pallas kernels, call(): pl.pallas_call(kernel, out_shape=out, in_specs=specs, out_specs=VMEM if s...  19.3 us
    all_to_all x1, blocking collectives, exchange(): return lax.all_to_all(v, 'rep', 0, 0)  14.4 us
    all_to_all x1, starting transfers between devices, exchange(): return lax.all_to_all(v, 'rep', 0, 0)  3.54 us
  transfers between devices with their start and end apart: 16, of which 9 were waited for; matrix products, arithmetic and copies ran while one was open for 2% of the time, Pallas kernels for 15%

profile of v3, /device:TPU:1, one launch (start us, length us, event | category | flops | bytes accessed | tf_op | source)
XLA Modules:
  0.0 120.3 jit_solution(3695283738432937516)
XLA Ops:
  0.6 8.4 %collective-permute-start = (bf16[1,128,512]{2,1,0:T(8,128)(2,1)}, bf16[1,128,512]{2,1,0:T(8,128)(2,1)S(1)}, u32[]{:S(2)}, u32[]{:S(2)}) collective-permute-start(bf16[1,128,512]{2,1,0:T(8,128)(2,1)} %weight.1), channel_id=1, source_target_pairs={{0,2},{1,3},{2,0},{3,1},{4,6},{5,7},{6,4},{7,5},{8,10},{9,11},{10,... | collective-permute-start | bytes 393224 | tf_op jit(solution)/shard_map/ppermute | solution.py:193
  9.1 1.3 %broadcast_in_dim.17.gain = bf16[1,4096]{1,0:T(2,128)(2,1)} reshape(bf16[4096]{0:T(1024)(128)(2,1)} %param.7) | data formatting | bytes 16384 | tf_op jit(solution)/shard_map/broadcast_in_dim | solution.py:190
  10.4 0.6 compare_select_fusion.3.place
  11.0 4.6 %norm.1 = (bf16[8,240,512]{2,1,0:T(8,128)(2,1)}, bf16[240,2304]{1,0:T(8,128)(2,1)}, f32[240,1]{1,0:T(8,128)}) custom-call(s32[16]{0:T(128)} %compare_select_fusion.3.place, bf16[240,4096]{1,0:T(8,128)(2,1)} %tok.1, bf16[1,4096]{1,0:T(2,128)(2,1)} %broadcast_in_dim.17.gain, bf16[240,512]{1,0:T(8,128)(2,1)} %cot.5), custom_call_target="tpu_custom_call" | custom-call | tf_op jit(solution)/shard_map/norm/pallas_call | solution.py:167
  15.6 6.1 %collective-permute-start.3 = (bf16[240,2304]{1,0:T(8,128)(2,1)}, bf16[240,2304]{1,0:T(8,128)(2,1)S(1)}, u32[]{:S(2)}, u32[]{:S(2)}) collective-permute-start(bf16[240,2304]{1,0:T(8,128)(2,1)} %get-tuple-element.38), channel_id=1, source_target_pairs={{0,1},{1,0},{2,3},{3,2},{4,5},{5,4},{6,7},{7,6},{8,9},{9,8},{10,11... | collective-permute-start | bytes 3317768 | tf_op jit(solution)/shard_map/ppermute | solution.py:193
  21.7 1.9 %collective-permute-start.1 = (bf16[2,128,512]{2,1,0:T(8,128)(2,1)S(1)}, bf16[2,128,512]{2,1,0:T(8,128)(2,1)S(1)}, u32[]{:S(2)}, u32[]{:S(2)}) collective-permute-start(bf16[2,128,512]{2,1,0:T(8,128)(2,1)S(1)} %pad_maximum_fusion.1), channel_id=1, source_target_pairs={{0,1},{1,0},{2,3},{3,2},{4,5},{5,4},{6,7},{7,6},{8,9},{9,8},{10,11... | collective-permute-start | bytes 786440 | tf_op jit(solution)/shard_map/ppermute | solution.py:193
  23.6 1.5 %collective-permute-done.1.other_core = bf16[2,128,512]{2,1,0:T(8,128)(2,1)S(1)} collective-permute-done((bf16[2,128,512]{2,1,0:T(8,128)(2,1)S(1)}, bf16[2,128,512]{2,1,0:T(8,128)(2,1)S(1)}, u32[]{:S(2)}, u32[]{:S(2)}) %collective-permute-start.1) | collective-permute-done | bytes 262176 | tf_op jit(solution)/shard_map/ppermute | solution.py:193
  25.1 0.6 join.1
  25.7 1.9 %collective-permute-start.2 = (bf16[512,512]{1,0:T(8,128)(2,1)S(1)}, bf16[512,512]{1,0:T(8,128)(2,1)S(1)}, u32[]{:S(2)}, u32[]{:S(2)}) collective-permute-start(bf16[512,512]{1,0:T(8,128)(2,1)S(1)} %bitcast.11), channel_id=1, source_target_pairs={{0,28},{1,5},{2,30},{3,7},{4,0},{5,9},{6,2},{7,11},{8,4},{9,13},{1... | collective-permute-start | bytes 1572872 | tf_op jit(solution)/shard_map/ppermute | solution.py:193
  27.7 0.0 collective-permute-done.3.got
  27.7 1.5 %copy-done = bf16[8,240,512]{2,1,0:T(8,128)(2,1)S(1)} copy-done((bf16[8,240,512]{2,1,0:T(8,128)(2,1)S(1)}, bf16[8,240,512]{2,1,0:T(8,128)(2,1)}, u32[]{:S(2)}) %copy-start) | copy-done | bytes 1966104
  29.2 1.8 %weight_grad.1 = (bf16[256,512]{1,0:T(8,128)(2,1)S(1)}, f32[512,512]{1,0:T(8,128)S(1)}, f32[512,512]{1,0:T(8,128)S(1)}, f32[512,512]{1,0:T(8,128)S(1)}, f32[512,512]{1,0:T(8,128)S(1)}) custom-call(s32[16]{0:T(128)S(1)} %copy-done.6, bf16[8,240,512]{2,1,0:T(8,128)(2,1)S(1)} %copy-done, bf16[240,512]{1,0:T(8,128)(2,1)S(1)} %copy-done.2, ...), custom_call_target="tpu_custom_call" | custom-call | tf_op jit(solution)/shard_map/weight_grad/pallas_call | solution.py:167
  31.1 2.9 %collective-permute-start.4 = (bf16[256,512]{1,0:T(8,128)(2,1)S(1)}, bf16[256,512]{1,0:T(8,128)(2,1)S(1)}, u32[]{:S(2)}, u32[]{:S(2)}) collective-permute-start(bf16[256,512]{1,0:T(8,128)(2,1)S(1)} %get-tuple-element.40), channel_id=1, source_target_pairs={{0,28},{1,5},{2,30},{3,7},{4,0},{5,9},{6,2},{7,11},{8,4},{9,13},{1... | collective-permute-start | bytes 786440 | tf_op jit(solution)/shard_map/ppermute | solution.py:193
  34.0 5.8 %collective-permute-done.2.earlier.w7 = bf16[512,512]{1,0:T(8,128)(2,1)S(1)} collective-permute-done((bf16[512,512]{1,0:T(8,128)(2,1)S(1)}, bf16[512,512]{1,0:T(8,128)(2,1)S(1)}, u32[]{:S(2)}, u32[]{:S(2)}) %collective-permute-start.2) | collective-permute-done | bytes 524320 | tf_op jit(solution)/shard_map/ppermute | solution.py:193
  39.8 2.8 %collective-permute-done.4.got = bf16[256,512]{1,0:T(8,128)(2,1)S(1)} collective-permute-done((bf16[256,512]{1,0:T(8,128)(2,1)S(1)}, bf16[256,512]{1,0:T(8,128)(2,1)S(1)}, u32[]{:S(2)}, u32[]{:S(2)}) %collective-permute-start.4) | collective-permute-done | bytes 262176 | tf_op jit(solution)/shard_map/ppermute | solution.py:193
  42.6 0.7 sum_3.1.earlier
  43.3 0.0 copy-start.5
  43.3 2.1 %collective-permute-start.6 = (bf16[512,512]{1,0:T(8,128)(2,1)S(1)}, bf16[512,512]{1,0:T(8,128)(2,1)S(1)}, u32[]{:S(2)}, u32[]{:S(2)}) collective-permute-start(bf16[512,512]{1,0:T(8,128)(2,1)S(1)} %sum_3.1.earlier), channel_id=1, source_target_pairs={{0,28},{1,5},{2,30},{3,7},{4,0},{5,9},{6,2},{7,11},{8,4},{9,13},{1... | collective-permute-start | bytes 1572872 | tf_op jit(solution)/shard_map/ppermute | solution.py:193
  45.3 2.0 %collective-permute-start.5 = (bf16[512,512]{1,0:T(8,128)(2,1)S(1)}, bf16[512,512]{1,0:T(8,128)(2,1)S(1)}, u32[]{:S(2)}, u32[]{:S(2)}) collective-permute-start(bf16[512,512]{1,0:T(8,128)(2,1)S(1)} %collective-permute-done.2.earlier.w7), channel_id=1, source_target_pairs={{0,28},{1,5},{2,30},{3,7},{4,0},{5,9},{6,2},{7,11},{8,4},{9,13},{1... | collective-permute-start | bytes 1572872 | tf_op jit(solution)/shard_map/ppermute | solution.py:193
  47.3 7.2 %collective-permute-done.6.got = bf16[512,512]{1,0:T(8,128)(2,1)S(1)} collective-permute-done((bf16[512,512]{1,0:T(8,128)(2,1)S(1)}, bf16[512,512]{1,0:T(8,128)(2,1)S(1)}, u32[]{:S(2)}, u32[]{:S(2)}) %collective-permute-start.6) | collective-permute-done | bytes 524320 | tf_op jit(solution)/shard_map/ppermute | solution.py:193
  54.5 0.1 sum_2.1
  54.7 1.9 %collective-permute-start.8 = (bf16[512,512]{1,0:T(8,128)(2,1)S(1)}, bf16[512,512]{1,0:T(8,128)(2,1)S(1)}, u32[]{:S(2)}, u32[]{:S(2)}) collective-permute-start(bf16[512,512]{1,0:T(8,128)(2,1)S(1)} %sum_2.1), channel_id=1, source_target_pairs={{0,28},{1,5},{2,30},{3,7},{4,0},{5,9},{6,2},{7,11},{8,4},{9,13},{1... | collective-permute-start | bytes 1572872 | tf_op jit(solution)/shard_map/ppermute | solution.py:193
  56.6 3.5 %collective-permute-done.5.w6 = bf16[512,512]{1,0:T(8,128)(2,1)S(1)} collective-permute-done((bf16[512,512]{1,0:T(8,128)(2,1)S(1)}, bf16[512,512]{1,0:T(8,128)(2,1)S(1)}, u32[]{:S(2)}, u32[]{:S(2)}) %collective-permute-start.5) | collective-permute-done | bytes 524320 | tf_op jit(solution)/shard_map/ppermute | solution.py:193
  60.2 1.9 %collective-permute-start.7 = (bf16[512,512]{1,0:T(8,128)(2,1)S(1)}, bf16[512,512]{1,0:T(8,128)(2,1)S(1)}, u32[]{:S(2)}, u32[]{:S(2)}) collective-permute-start(bf16[512,512]{1,0:T(8,128)(2,1)S(1)} %collective-permute-done.5.w6), channel_id=1, source_target_pairs={{0,28},{1,5},{2,30},{3,7},{4,0},{5,9},{6,2},{7,11},{8,4},{9,13},{1... | collective-permute-start | bytes 1572872 | tf_op jit(solution)/shard_map/ppermute | solution.py:193
  62.1 14.4 %all_to_all.10.pieces = bf16[16,16,512]{2,1,0:T(8,128)(2,1)S(1)} all-to-all(bf16[16,16,512]{2,1,0:T(8,128)(2,1)S(1)} %bitcast.20), channel_id=1, replica_groups=mesh['rep'=16,'fsdp'=32] {'rep'}, dimensions={0} | all-to-all | bytes 524288 | tf_op jit(solution)/shard_map/all_to_all | solution.py:203
  76.5 1.3 %choose.1.earlier = bf16[16,16,512]{2,1,0:T(8,128)(2,1)} custom-call(s32[16]{0:T(128)S(1)} %copy-done.7, bf16[16,16,512]{2,1,0:T(8,128)(2,1)S(1)} %all_to_all.10.pieces), custom_call_target="tpu_custom_call" | custom-call | tf_op jit(solution)/shard_map/choose/pallas_call | solution.py:167
  77.8 0.0 collective-permute-done.8.got
  77.8 0.1 sum_1.1
  77.9 0.0 collective-permute-done.7.w5
  78.0 1.3 %pad_maximum_fusion = bf16[3,512,512]{2,1,0:T(8,128)(2,1)} fusion(bf16[1,512,512]{2,1,0:T(8,128)(2,1)S(1)} %bitcast.18, bf16[1,512,512]{2,1,0:T(8,128)(2,1)S(1)} %bitcast.19, bf16[1,512,512]{2,1,0:T(8,128)(2,1)S(1)} %bitcast.10), kind=kLoop, calls=%fused_computation | loop fusion | flops 1572864 | bytes 3145728 | tf_op jit(solution)/shard_map/stack | solution.py:269
  79.3 9.0 %collective-permute-start.10 = (bf16[3,512,512]{2,1,0:T(8,128)(2,1)}, bf16[3,512,512]{2,1,0:T(8,128)(2,1)}, u32[]{:S(2)}, u32[]{:S(2)}) collective-permute-start(bf16[3,512,512]{2,1,0:T(8,128)(2,1)} %pad_maximum_fusion), channel_id=1, source_target_pairs={{0,1},{1,0},{2,3},{3,2},{4,5},{5,4},{6,7},{7,6},{8,9},{9,8},{10,11... | collective-permute-start | bytes 4718600 | tf_op jit(solution)/shard_map/ppermute | solution.py:193
  88.3 1.9 %collective-permute-start.11 = (bf16[512,512]{1,0:T(8,128)(2,1)S(1)}, bf16[512,512]{1,0:T(8,128)(2,1)S(1)}, u32[]{:S(2)}, u32[]{:S(2)}) collective-permute-start(bf16[512,512]{1,0:T(8,128)(2,1)S(1)} %sum_1.1), channel_id=1, source_target_pairs={{0,28},{1,5},{2,30},{3,7},{4,0},{5,9},{6,2},{7,11},{8,4},{9,13},{1... | collective-permute-start | bytes 1572872 | tf_op jit(solution)/shard_map/ppermute | solution.py:193
  90.2 0.7 constant_dynamic-slice_fusion
  90.9 1.9 %collective-permute-start.9 = (bf16[256,512]{1,0:T(8,128)(2,1)}, bf16[256,512]{1,0:T(8,128)(2,1)S(1)}, u32[]{:S(2)}, u32[]{:S(2)}) collective-permute-start(bf16[256,512]{1,0:T(8,128)(2,1)} %constant_dynamic-slice_fusion), channel_id=1, source_target_pairs={{0,28},{1,5},{2,30},{3,7},{4,0},{5,9},{6,2},{7,11},{8,4},{9,13},{1... | collective-permute-start | bytes 786440 | tf_op jit(solution)/shard_map/ppermute | solution.py:193
  92.9 3.5 %all-to-all-start.1 = ((bf16[16,16,512]{2,1,0:T(8,128)(2,1)}), bf16[16,16,512]{2,1,0:T(8,128)(2,1)S(1)}, u32[]{:S(2)}, u32[]{:S(2)}) async-start(bf16[16,16,512]{2,1,0:T(8,128)(2,1)} %choose.1.earlier), calls=%async_computation.1 | async-start | bytes 524288 | tf_op jit(solution)/shard_map/all_to_all | solution.py:203
  96.4 3.0 %collective-permute-done.11 = bf16[512,512]{1,0:T(8,128)(2,1)S(1)} collective-permute-done((bf16[512,512]{1,0:T(8,128)(2,1)S(1)}, bf16[512,512]{1,0:T(8,128)(2,1)S(1)}, u32[]{:S(2)}, u32[]{:S(2)}) %collective-permute-start.11) | collective-permute-done | bytes 524320 | tf_op jit(solution)/shard_map/ppermute | solution.py:193
  99.4 0.6 core_sum.1
  100.0 1.9 %collective-permute-start.12 = (bf16[2,128,512]{2,1,0:T(8,128)(2,1)S(1)}, bf16[2,128,512]{2,1,0:T(8,128)(2,1)S(1)}, u32[]{:S(2)}, u32[]{:S(2)}) collective-permute-start(bf16[2,128,512]{2,1,0:T(8,128)(2,1)S(1)} %get-tuple-element.51), channel_id=1, source_target_pairs={{0,1},{1,0},{2,3},{3,2},{4,5},{5,4},{6,7},{7,6},{8,9},{9,8},{10,11... | collective-permute-start | bytes 786440 | tf_op jit(solution)/shard_map/ppermute | solution.py:193
  102.0 0.5 collective-permute-done.9.h4
  102.5 1.9 %collective-permute-start.13 = (bf16[256,512]{1,0:T(8,128)(2,1)S(1)}, bf16[256,512]{1,0:T(8,128)(2,1)S(1)}, u32[]{:S(2)}, u32[]{:S(2)}) collective-permute-start(bf16[256,512]{1,0:T(8,128)(2,1)S(1)} %collective-permute-done.9.h4), channel_id=1, source_target_pairs={{0,1},{1,0},{2,3},{3,2},{4,5},{5,4},{6,7},{7,6},{8,9},{9,8},{10,11... | collective-permute-start | bytes 786440 | tf_op jit(solution)/shard_map/ppermute | solution.py:193
  104.4 0.6 y_sum.1
  105.0 0.9 collective-permute-done.13.swapped4
  105.9 4.8 %collective-permute-start.14 = (bf16[1,128,512]{2,1,0:T(8,128)(2,1)S(1)}, bf16[1,128,512]{2,1,0:T(8,128)(2,1)S(1)}, u32[]{:S(2)}, u32[]{:S(2)}) collective-permute-start(bf16[1,128,512]{2,1,0:T(8,128)(2,1)S(1)} %get-tuple-element.56), channel_id=1, source_target_pairs={{0,2},{1,3},{2,0},{3,1},{4,6},{5,7},{6,4},{7,5},{8,10},{9,11},{10,... | collective-permute-start | bytes 393224 | tf_op jit(solution)/shard_map/ppermute | solution.py:193
  110.8 0.0 collective-permute-done.10.swapped
  110.8 8.0 %token_grad.1 = (bf16[240,512]{1,0:T(8,128)(2,1)}, bf16[240,4096]{1,0:T(8,128)(2,1)}) custom-call(s32[16]{0:T(128)} %compare_select_fusion.3.place, bf16[240,4096]{1,0:T(8,128)(2,1)} %tok.1, bf16[1,4096]{1,0:T(2,128)(2,1)} %broadcast_in_dim.17.gain, f32[240,1]{1,0:T(8,128)} %get-tuple-element.34.inverse, bf16[8,240,512]{2,1,0:T(8,128)(2,1)} %get-tuple-element.35.normed, ...), custom_call_target="tpu_custom_call" | custom-call | tf_op jit(solution)/shard_map/token_grad/pallas_call | solution.py:167
  118.8 0.7 collective-permute-done.14.got
  119.5 0.0 all-to-all-done.1
  119.5 0.8 update.1
  (26 shorter events, 0.1 us)
Async XLA Ops:
  0.6 21.0 %copy-start.4 = (bf16[1,128,512]{2,1,0:T(8,128)(2,1)S(1)}, bf16[1,128,512]{2,1,0:T(8,128)(2,1)}, u32[]{:S(2)}) copy-start(bf16[1,128,512]{2,1,0:T(8,128)(2,1)} %weight.1) | copy-start | bytes 393220
  0.6 15.0 %collective-permute-start = (bf16[1,128,512]{2,1,0:T(8,128)(2,1)}, bf16[1,128,512]{2,1,0:T(8,128)(2,1)S(1)}, u32[]{:S(2)}, u32[]{:S(2)}) collective-permute-start(bf16[1,128,512]{2,1,0:T(8,128)(2,1)} %weight.1), channel_id=1, source_target_pairs={{0,2},{1,3},{2,0},{3,1},{4,6},{5,7},{6,4},{7,5},{8,10},{9,11},{10,... | collective-permute-start | bytes 393224 | tf_op jit(solution)/shard_map/ppermute | solution.py:193
  11.0 14.2 %copy-start.6 = (s32[16]{0:T(128)S(1)}, s32[16]{0:T(128)}, u32[]{:S(2)}) copy-start(s32[16]{0:T(128)} %compare_select_fusion.3.place) | copy-start | bytes 196
  11.0 16.7 %copy-start.2 = (bf16[240,512]{1,0:T(8,128)(2,1)S(1)}, bf16[240,512]{1,0:T(8,128)(2,1)}, u32[]{:S(2)}) copy-start(bf16[240,512]{1,0:T(8,128)(2,1)} %cot.5) | copy-start | bytes 737284
  15.6 12.1 %collective-permute-start.3 = (bf16[240,2304]{1,0:T(8,128)(2,1)}, bf16[240,2304]{1,0:T(8,128)(2,1)S(1)}, u32[]{:S(2)}, u32[]{:S(2)}) collective-permute-start(bf16[240,2304]{1,0:T(8,128)(2,1)} %get-tuple-element.38), channel_id=1, source_target_pairs={{0,1},{1,0},{2,3},{3,2},{4,5},{5,4},{6,7},{7,6},{8,9},{9,8},{10,11... | collective-permute-start | bytes 3317768 | tf_op jit(solution)/shard_map/ppermute | solution.py:193
  21.7 3.4 %collective-permute-start.1 = (bf16[2,128,512]{2,1,0:T(8,128)(2,1)S(1)}, bf16[2,128,512]{2,1,0:T(8,128)(2,1)S(1)}, u32[]{:S(2)}, u32[]{:S(2)}) collective-permute-start(bf16[2,128,512]{2,1,0:T(8,128)(2,1)S(1)} %pad_maximum_fusion.1), channel_id=1, source_target_pairs={{0,1},{1,0},{2,3},{3,2},{4,5},{5,4},{6,7},{7,6},{8,9},{9,8},{10,11... | collective-permute-start | bytes 786440 | tf_op jit(solution)/shard_map/ppermute | solution.py:193
  25.7 5.4 %copy-start.3 = (bf16[4,128,512]{2,1,0:T(8,128)(2,1)}, bf16[4,128,512]{2,1,0:T(8,128)(2,1)S(1)}, u32[]{:S(2)}) copy-start(bf16[4,128,512]{2,1,0:T(8,128)(2,1)S(1)} %join.1) | copy-start | bytes 1572868
  25.7 14.0 %collective-permute-start.2 = (bf16[512,512]{1,0:T(8,128)(2,1)S(1)}, bf16[512,512]{1,0:T(8,128)(2,1)S(1)}, u32[]{:S(2)}, u32[]{:S(2)}) collective-permute-start(bf16[512,512]{1,0:T(8,128)(2,1)S(1)} %bitcast.11), channel_id=1, source_target_pairs={{0,28},{1,5},{2,30},{3,7},{4,0},{5,9},{6,2},{7,11},{8,4},{9,13},{1... | collective-permute-start | bytes 1572872 | tf_op jit(solution)/shard_map/ppermute | solution.py:193
  27.7 1.5 %copy-start = (bf16[8,240,512]{2,1,0:T(8,128)(2,1)S(1)}, bf16[8,240,512]{2,1,0:T(8,128)(2,1)}, u32[]{:S(2)}) copy-start(bf16[8,240,512]{2,1,0:T(8,128)(2,1)} %get-tuple-element.35.normed) | copy-start | bytes 5898244
  31.1 11.5 %collective-permute-start.4 = (bf16[256,512]{1,0:T(8,128)(2,1)S(1)}, bf16[256,512]{1,0:T(8,128)(2,1)S(1)}, u32[]{:S(2)}, u32[]{:S(2)}) collective-permute-start(bf16[256,512]{1,0:T(8,128)(2,1)S(1)} %get-tuple-element.40), channel_id=1, source_target_pairs={{0,28},{1,5},{2,30},{3,7},{4,0},{5,9},{6,2},{7,11},{8,4},{9,13},{1... | collective-permute-start | bytes 786440 | tf_op jit(solution)/shard_map/ppermute | solution.py:193
  39.8 38.2 %copy-start.1 = (bf16[512,512]{1,0:T(8,128)(2,1)}, bf16[512,512]{1,0:T(8,128)(2,1)S(1)}, u32[]{:S(2)}) copy-start(bf16[512,512]{1,0:T(8,128)(2,1)S(1)} %collective-permute-done.2.earlier.w7) | copy-start | bytes 1572868
  43.3 18.8 %copy-start.5 = (bf16[1,128,512]{2,1,0:T(8,128)(2,1)S(1)}, bf16[1,128,512]{2,1,0:T(8,128)(2,1)}, u32[]{:S(2)}) copy-start(bf16[1,128,512]{2,1,0:T(8,128)(2,1)} %momentum.1) | copy-start | bytes 393220
  43.3 11.3 %collective-permute-start.6 = (bf16[512,512]{1,0:T(8,128)(2,1)S(1)}, bf16[512,512]{1,0:T(8,128)(2,1)S(1)}, u32[]{:S(2)}, u32[]{:S(2)}) collective-permute-start(bf16[512,512]{1,0:T(8,128)(2,1)S(1)} %sum_3.1.earlier), channel_id=1, source_target_pairs={{0,28},{1,5},{2,30},{3,7},{4,0},{5,9},{6,2},{7,11},{8,4},{9,13},{1... | collective-permute-start | bytes 1572872 | tf_op jit(solution)/shard_map/ppermute | solution.py:193
  45.3 14.8 %collective-permute-start.5 = (bf16[512,512]{1,0:T(8,128)(2,1)S(1)}, bf16[512,512]{1,0:T(8,128)(2,1)S(1)}, u32[]{:S(2)}, u32[]{:S(2)}) collective-permute-start(bf16[512,512]{1,0:T(8,128)(2,1)S(1)} %collective-permute-done.2.earlier.w7), channel_id=1, source_target_pairs={{0,28},{1,5},{2,30},{3,7},{4,0},{5,9},{6,2},{7,11},{8,4},{9,13},{1... | collective-permute-start | bytes 1572872 | tf_op jit(solution)/shard_map/ppermute | solution.py:193
  54.5 22.0 %copy-start.7 = (s32[16]{0:T(128)S(1)}, s32[16]{0:T(128)}, u32[]{:S(2)}) copy-start(s32[16]{0:T(128)} %matching.1) | copy-start | bytes 196
  54.7 23.1 %collective-permute-start.8 = (bf16[512,512]{1,0:T(8,128)(2,1)S(1)}, bf16[512,512]{1,0:T(8,128)(2,1)S(1)}, u32[]{:S(2)}, u32[]{:S(2)}) collective-permute-start(bf16[512,512]{1,0:T(8,128)(2,1)S(1)} %sum_2.1), channel_id=1, source_target_pairs={{0,28},{1,5},{2,30},{3,7},{4,0},{5,9},{6,2},{7,11},{8,4},{9,13},{1... | collective-permute-start | bytes 1572872 | tf_op jit(solution)/shard_map/ppermute | solution.py:193
  60.2 17.8 %copy-start.9 = (bf16[512,512]{1,0:T(8,128)(2,1)}, bf16[512,512]{1,0:T(8,128)(2,1)S(1)}, u32[]{:S(2)}) copy-start(bf16[512,512]{1,0:T(8,128)(2,1)S(1)} %collective-permute-done.5.w6) | copy-start | bytes 1572868
  60.2 17.8 %collective-permute-start.7 = (bf16[512,512]{1,0:T(8,128)(2,1)S(1)}, bf16[512,512]{1,0:T(8,128)(2,1)S(1)}, u32[]{:S(2)}, u32[]{:S(2)}) collective-permute-start(bf16[512,512]{1,0:T(8,128)(2,1)S(1)} %collective-permute-done.5.w6), channel_id=1, source_target_pairs={{0,28},{1,5},{2,30},{3,7},{4,0},{5,9},{6,2},{7,11},{8,4},{9,13},{1... | collective-permute-start | bytes 1572872 | tf_op jit(solution)/shard_map/ppermute | solution.py:193
  77.9 12.3 %copy-start.8 = (bf16[512,512]{1,0:T(8,128)(2,1)}, bf16[512,512]{1,0:T(8,128)(2,1)S(1)}, u32[]{:S(2)}) copy-start(bf16[512,512]{1,0:T(8,128)(2,1)S(1)} %collective-permute-done.7.w5) | copy-start | bytes 1572868
  79.3 31.5 %collective-permute-start.10 = (bf16[3,512,512]{2,1,0:T(8,128)(2,1)}, bf16[3,512,512]{2,1,0:T(8,128)(2,1)}, u32[]{:S(2)}, u32[]{:S(2)}) collective-permute-start(bf16[3,512,512]{2,1,0:T(8,128)(2,1)} %pad_maximum_fusion), channel_id=1, source_target_pairs={{0,1},{1,0},{2,3},{3,2},{4,5},{5,4},{6,7},{7,6},{8,9},{9,8},{10,11... | collective-permute-start | bytes 4718600 | tf_op jit(solution)/shard_map/ppermute | solution.py:193
  88.3 11.1 %collective-permute-start.11 = (bf16[512,512]{1,0:T(8,128)(2,1)S(1)}, bf16[512,512]{1,0:T(8,128)(2,1)S(1)}, u32[]{:S(2)}, u32[]{:S(2)}) collective-permute-start(bf16[512,512]{1,0:T(8,128)(2,1)S(1)} %sum_1.1), channel_id=1, source_target_pairs={{0,28},{1,5},{2,30},{3,7},{4,0},{5,9},{6,2},{7,11},{8,4},{9,13},{1... | collective-permute-start | bytes 1572872 | tf_op jit(solution)/shard_map/ppermute | solution.py:193
  90.9 11.6 %collective-permute-start.9 = (bf16[256,512]{1,0:T(8,128)(2,1)}, bf16[256,512]{1,0:T(8,128)(2,1)S(1)}, u32[]{:S(2)}, u32[]{:S(2)}) collective-permute-start(bf16[256,512]{1,0:T(8,128)(2,1)} %constant_dynamic-slice_fusion), channel_id=1, source_target_pairs={{0,28},{1,5},{2,30},{3,7},{4,0},{5,9},{6,2},{7,11},{8,4},{9,13},{1... | collective-permute-start | bytes 786440 | tf_op jit(solution)/shard_map/ppermute | solution.py:193
  92.9 26.6 %all-to-all-start.1 = ((bf16[16,16,512]{2,1,0:T(8,128)(2,1)}), bf16[16,16,512]{2,1,0:T(8,128)(2,1)S(1)}, u32[]{:S(2)}, u32[]{:S(2)}) async-start(bf16[16,16,512]{2,1,0:T(8,128)(2,1)} %choose.1.earlier), calls=%async_computation.1 | async-start | bytes 524288 | tf_op jit(solution)/shard_map/all_to_all | solution.py:203
  100.0 4.4 %collective-permute-start.12 = (bf16[2,128,512]{2,1,0:T(8,128)(2,1)S(1)}, bf16[2,128,512]{2,1,0:T(8,128)(2,1)S(1)}, u32[]{:S(2)}, u32[]{:S(2)}) collective-permute-start(bf16[2,128,512]{2,1,0:T(8,128)(2,1)S(1)} %get-tuple-element.51), channel_id=1, source_target_pairs={{0,1},{1,0},{2,3},{3,2},{4,5},{5,4},{6,7},{7,6},{8,9},{9,8},{10,11... | collective-permute-start | bytes 786440 | tf_op jit(solution)/shard_map/ppermute | solution.py:193
  102.5 8.3 %copy-start.10 = (bf16[256,512]{1,0:T(8,128)(2,1)}, bf16[256,512]{1,0:T(8,128)(2,1)S(1)}, u32[]{:S(2)}) copy-start(bf16[256,512]{1,0:T(8,128)(2,1)S(1)} %collective-permute-done.9.h4) | copy-start | bytes 786436
  102.5 3.4 %collective-permute-start.13 = (bf16[256,512]{1,0:T(8,128)(2,1)S(1)}, bf16[256,512]{1,0:T(8,128)(2,1)S(1)}, u32[]{:S(2)}, u32[]{:S(2)}) collective-permute-start(bf16[256,512]{1,0:T(8,128)(2,1)S(1)} %collective-permute-done.9.h4), channel_id=1, source_target_pairs={{0,1},{1,0},{2,3},{3,2},{4,5},{5,4},{6,7},{7,6},{8,9},{9,8},{10,11... | collective-permute-start | bytes 786440 | tf_op jit(solution)/shard_map/ppermute | solution.py:193
  105.9 4.9 %copy-start.11 = (bf16[256,512]{1,0:T(8,128)(2,1)}, bf16[256,512]{1,0:T(8,128)(2,1)S(1)}, u32[]{:S(2)}) copy-start(bf16[256,512]{1,0:T(8,128)(2,1)S(1)} %collective-permute-done.13.swapped4) | copy-start | bytes 786436
  105.9 13.6 %collective-permute-start.14 = (bf16[1,128,512]{2,1,0:T(8,128)(2,1)S(1)}, bf16[1,128,512]{2,1,0:T(8,128)(2,1)S(1)}, u32[]{:S(2)}, u32[]{:S(2)}) collective-permute-start(bf16[1,128,512]{2,1,0:T(8,128)(2,1)S(1)} %get-tuple-element.56), channel_id=1, source_target_pairs={{0,2},{1,3},{2,0},{3,1},{4,6},{5,7},{6,4},{7,5},{8,10},{9,11},{10,... | collective-permute-start | bytes 393224 | tf_op jit(solution)/shard_map/ppermute | solution.py:193

commit v4 on v3

--- a/solution.py
+++ b/solution.py
@@ -28,7 +28,8 @@
     return pl.ds(pl.multiple_of(place[slot] * B, B), B)
 
 
-def norm_kernel(place, tok_in, gain, cot, normed, send, inverse, tok, sems):
+def norm_kernel(place, tok_in, gain_in, cot, normed, send, inverse, tok, gain, sems):
+    gain[...] = gain_in[...].astype(F32).reshape(gain.shape)
     count = tok.shape[0]
     chunk = 80 if count % 80 == 0 else count
     starts = range(0, count, chunk)
@@ -52,7 +53,7 @@
         inverse[rows, :] = scale
         for j in range(NB):
             where = columns(place, j)
-            value = (tok[rows, where].astype(F32) * scale * gain[:, where].astype(F32)).astype(
+            value = (tok[rows, where].astype(F32) * scale * gain[:, where]).astype(
                 BF16
             )
             normed[j, rows, :] = value
@@ -82,32 +83,41 @@
 
 
 def token_kernel(
-    place, tok, gain, inverse, normed, cot, w0, w7, w6, w5, h4, swapped, swapped4, keys, grad, w4, back
+    place, tok_in, gain_in, inverse, normed_in, cot, w0, w7, w6, w5, h4, swapped, swapped4,
+    keys, grad, w4, back, tok, normed, gain, sems,
 ):
+    gain[...] = gain_in[...].astype(F32).reshape(gain.shape)
+    load_normed = pltpu.make_async_copy(normed_in, normed, sems.at[0])
+    load_tok = pltpu.make_async_copy(tok_in, tok, sems.at[1])
+    load_normed.start()
+    load_tok.start()
     here = pl.multiple_of(place[NB] * H, H)
     there = pl.multiple_of((1 - place[NB]) * H, H)
     w4[pl.ds(here, H), :] = h4[...]
     w4[pl.ds(there, H), :] = swapped4[...]
     blocks = (w0, swapped.at[0], swapped.at[1], swapped.at[2], w4, w5, w6, w7)
     mine = cot[...]
+    for j, block in enumerate(blocks):
+        back[j] = (
+            lax.dot_general(mine, block[...], (((1,), (1,)), ((), ())), preferred_element_type=F32)
+            * SCALE
+        ).astype(BF16)
+    load_normed.wait()
     total = jnp.zeros(keys.shape, F32)
+    for j, block in enumerate(blocks):
+        total += jnp.dot(normed[j], block[...], preferred_element_type=F32)
+    keys[...] = (total * SCALE).astype(BF16)
+    load_tok.wait()
     mixed = jnp.zeros((tok.shape[0], 1), F32)
-    for j, block in enumerate(blocks):
+    for j in range(NB):
         where = columns(place, j)
-        w = block[...]
-        total += jnp.dot(normed[j], w, preferred_element_type=F32)
-        down = (
-            lax.dot_general(mine, w, (((1,), (1,)), ((), ())), preferred_element_type=F32) * SCALE
-        ).astype(BF16)
-        back[j] = down
-        up = down.astype(F32) * gain[:, where].astype(F32)
+        up = back[j].astype(F32) * gain[:, where]
         mixed += jnp.sum(up * tok[:, where].astype(F32), axis=1, keepdims=True)
-    keys[...] = (total * SCALE).astype(BF16)
     scale = inverse[...]
     factor = scale * scale * (mixed * (1.0 / D))
     for j in range(NB):
         where = columns(place, j)
-        up = back[j].astype(F32) * gain[:, where].astype(F32)
+        up = back[j].astype(F32) * gain[:, where]
         grad[:, where] = (scale * (up - tok[:, where].astype(F32) * factor)).astype(BF16)
 
 
@@ -187,7 +197,7 @@
     place = jnp.where(lane == NB, core, place)
     place = jnp.where(lane == NB + 1, (me >> 1) & 1, place)
     place = jnp.where(lane == NB + 2, group >> 2, place)
-    gain = norm_gain[None]
+    gain = norm_gain
 
     def along(v, perm):
         return lax.ppermute(v, "fsdp", perm)
@@ -213,7 +223,11 @@
         tokens,
         gain,
         key_grad,
-        scratch=[pltpu.VMEM((rows, D), BF16), pltpu.SemaphoreType.DMA((4,))],
+        scratch=[
+            pltpu.VMEM((rows, D), BF16),
+            pltpu.VMEM((1, D), F32),
+            pltpu.SemaphoreType.DMA((4,)),
+        ],
         vmem=56,
     )
     both = jnp.concatenate([after(weight, inverse)[0][0], momentum[0]], axis=0)
@@ -295,7 +309,7 @@
         token_kernel,
         "token_grad",
         (shape((rows, K), BF16), shape((rows, D), BF16)),
-        [SMEM] + [VMEM] * 12,
+        [SMEM, ANY, VMEM, VMEM, ANY] + [VMEM] * 8,
         place,
         tokens,
         gain,
@@ -309,7 +323,14 @@
         h4,
         swapped,
         swapped4,
-        scratch=[pltpu.VMEM((B, K), BF16), pltpu.VMEM((NB, rows, B), BF16)],
+        scratch=[
+            pltpu.VMEM((B, K), BF16),
+            pltpu.VMEM((NB, rows, B), BF16),
+            pltpu.VMEM((rows, D), BF16),
+            pltpu.VMEM((NB, rows, B), BF16),
+            pltpu.VMEM((1, D), F32),
+            pltpu.SemaphoreType.DMA((2,)),
+        ],
         vmem=56,
     )
     keys, token_grad, got = after(keys, token_grad, got)

time: 121 us -> 121 us (level)
  blocking collectives: 14.4 us -> 15.8 us
  local copies, waits for them, and re-layouts: 3.63 us -> 2.31 us
    all_to_all x1, blocking collectives: 14.4 us -> 15.8 us  [exchange(): return lax.all_to_all(v, 'rep', 0, 0)]
    broadcast_in_dim x1 -> x0, local copies, waits for them, and re-layouts: 1.31 us -> none  [per_device(): gain = norm_gain[None]]
  transfers between devices with their start and end apart: 16 -> 16, of which waited for: 9 -> 9; matrix products, arithmetic and copies ran while one was open for 2% -> 1% of each run, Pallas kernels for 15% -> 15%
where the time goes in v4:
time: 121 us; the launch traced here: 120 us
  starting transfers between devices  54.5 us (45%)
  waiting for transfers between devices  25.6 us (21%)
  Pallas kernels  19.3 us (16%)
  blocking collectives  15.8 us (13%)
  local copies, waits for them, and re-layouts  2.31 us (2%)
  other arithmetic  1.88 us (2%)
    ppermute x15, starting transfers between devices, along(): return lax.ppermute(v, 'fsdp', perm)  50.9 us
    ppermute x15, waiting for transfers between devices, along(): return lax.ppermute(v, 'fsdp', perm)  25.6 us
    pallas_call x11, Pallas kernels, call(): pl.pallas_call(kernel, out_shape=out, in_specs=specs, out_specs=VMEM if s...  19.3 us
    all_to_all x1, blocking collectives, exchange(): return lax.all_to_all(v, 'rep', 0, 0)  15.8 us
    all_to_all x1, starting transfers between devices, exchange(): return lax.all_to_all(v, 'rep', 0, 0)  3.54 us
  transfers between devices with their start and end apart: 16, of which 9 were waited for; matrix products, arithmetic and copies ran while one was open for 1% of the time, Pallas kernels for 15%

profile of v4, /device:TPU:1, one launch (start us, length us, event | category | flops | bytes accessed | tf_op | source)
XLA Modules:
  0.0 120.3 jit_solution(7331632578511532256)
XLA Ops:
  0.6 8.4 %collective-permute-start = (bf16[1,128,512]{2,1,0:T(8,128)(2,1)}, bf16[1,128,512]{2,1,0:T(8,128)(2,1)S(1)}, u32[]{:S(2)}, u32[]{:S(2)}) collective-permute-start(bf16[1,128,512]{2,1,0:T(8,128)(2,1)} %weight.1), channel_id=1, source_target_pairs={{0,2},{1,3},{2,0},{3,1},{4,6},{5,7},{6,4},{7,5},{8,10},{9,11},{10,... | collective-permute-start | bytes 393224 | tf_op jit(solution)/shard_map/ppermute | solution.py:203
  9.1 0.5 compare_select_fusion.3.place
  9.6 4.6 %norm.1 = (bf16[8,240,512]{2,1,0:T(8,128)(2,1)}, bf16[240,2304]{1,0:T(8,128)(2,1)}, f32[240,1]{1,0:T(8,128)}) custom-call(s32[16]{0:T(128)} %compare_select_fusion.3.place, bf16[240,4096]{1,0:T(8,128)(2,1)} %tok_in.3, bf16[4096]{0:T(1024)(128)(2,1)} %gain_in.3, bf16[240,512]{1,0:T(8,128)(2,1)} %cot.5), custom_call_target="tpu_custom_call" | custom-call | tf_op jit(solution)/shard_map/norm/pallas_call | solution.py:177
  14.2 0.0 collective-permute-done.other_y
  14.2 7.4 %collective-permute-start.3 = (bf16[240,2304]{1,0:T(8,128)(2,1)}, bf16[240,2304]{1,0:T(8,128)(2,1)S(1)}, u32[]{:S(2)}, u32[]{:S(2)}) collective-permute-start(bf16[240,2304]{1,0:T(8,128)(2,1)} %get-tuple-element.38), channel_id=1, source_target_pairs={{0,1},{1,0},{2,3},{3,2},{4,5},{5,4},{6,7},{7,6},{8,9},{9,8},{10,11... | collective-permute-start | bytes 3317768 | tf_op jit(solution)/shard_map/ppermute | solution.py:203
  21.7 1.9 %collective-permute-start.1 = (bf16[2,128,512]{2,1,0:T(8,128)(2,1)S(1)}, bf16[2,128,512]{2,1,0:T(8,128)(2,1)S(1)}, u32[]{:S(2)}, u32[]{:S(2)}) collective-permute-start(bf16[2,128,512]{2,1,0:T(8,128)(2,1)S(1)} %pad_maximum_fusion.1), channel_id=1, source_target_pairs={{0,1},{1,0},{2,3},{3,2},{4,5},{5,4},{6,7},{7,6},{8,9},{9,8},{10,11... | collective-permute-start | bytes 786440 | tf_op jit(solution)/shard_map/ppermute | solution.py:203
  23.6 1.5 %collective-permute-done.1.other_core = bf16[2,128,512]{2,1,0:T(8,128)(2,1)S(1)} collective-permute-done((bf16[2,128,512]{2,1,0:T(8,128)(2,1)S(1)}, bf16[2,128,512]{2,1,0:T(8,128)(2,1)S(1)}, u32[]{:S(2)}, u32[]{:S(2)}) %collective-permute-start.1) | collective-permute-done | bytes 262176 | tf_op jit(solution)/shard_map/ppermute | solution.py:203
  25.1 0.6 join.1
  25.7 1.9 %collective-permute-start.2 = (bf16[512,512]{1,0:T(8,128)(2,1)S(1)}, bf16[512,512]{1,0:T(8,128)(2,1)S(1)}, u32[]{:S(2)}, u32[]{:S(2)}) collective-permute-start(bf16[512,512]{1,0:T(8,128)(2,1)S(1)} %bitcast.11), channel_id=1, source_target_pairs={{0,28},{1,5},{2,30},{3,7},{4,0},{5,9},{6,2},{7,11},{8,4},{9,13},{1... | collective-permute-start | bytes 1572872 | tf_op jit(solution)/shard_map/ppermute | solution.py:203
  27.7 0.0 collective-permute-done.3.got
  27.7 1.5 %copy-done = bf16[8,240,512]{2,1,0:T(8,128)(2,1)S(1)} copy-done((bf16[8,240,512]{2,1,0:T(8,128)(2,1)S(1)}, bf16[8,240,512]{2,1,0:T(8,128)(2,1)}, u32[]{:S(2)}) %copy-start) | copy-done | bytes 1966104
  29.2 1.8 %weight_grad.1 = (bf16[256,512]{1,0:T(8,128)(2,1)S(1)}, f32[512,512]{1,0:T(8,128)S(1)}, f32[512,512]{1,0:T(8,128)S(1)}, f32[512,512]{1,0:T(8,128)S(1)}, f32[512,512]{1,0:T(8,128)S(1)}) custom-call(s32[16]{0:T(128)S(1)} %copy-done.6, bf16[8,240,512]{2,1,0:T(8,128)(2,1)S(1)} %copy-done, bf16[240,512]{1,0:T(8,128)(2,1)S(1)} %copy-done.2, ...), custom_call_target="tpu_custom_call" | custom-call | tf_op jit(solution)/shard_map/weight_grad/pallas_call | solution.py:177
  31.1 1.9 %collective-permute-start.4 = (bf16[256,512]{1,0:T(8,128)(2,1)S(1)}, bf16[256,512]{1,0:T(8,128)(2,1)S(1)}, u32[]{:S(2)}, u32[]{:S(2)}) collective-permute-start(bf16[256,512]{1,0:T(8,128)(2,1)S(1)} %get-tuple-element.40), channel_id=1, source_target_pairs={{0,28},{1,5},{2,30},{3,7},{4,0},{5,9},{6,2},{7,11},{8,4},{9,13},{1... | collective-permute-start | bytes 786440 | tf_op jit(solution)/shard_map/ppermute | solution.py:203
  33.0 5.4 %collective-permute-done.2.earlier.w7 = bf16[512,512]{1,0:T(8,128)(2,1)S(1)} collective-permute-done((bf16[512,512]{1,0:T(8,128)(2,1)S(1)}, bf16[512,512]{1,0:T(8,128)(2,1)S(1)}, u32[]{:S(2)}, u32[]{:S(2)}) %collective-permute-start.2) | collective-permute-done | bytes 524320 | tf_op jit(solution)/shard_map/ppermute | solution.py:203
  38.4 2.8 %collective-permute-done.4.got = bf16[256,512]{1,0:T(8,128)(2,1)S(1)} collective-permute-done((bf16[256,512]{1,0:T(8,128)(2,1)S(1)}, bf16[256,512]{1,0:T(8,128)(2,1)S(1)}, u32[]{:S(2)}, u32[]{:S(2)}) %collective-permute-start.4) | collective-permute-done | bytes 262176 | tf_op jit(solution)/shard_map/ppermute | solution.py:203
  41.2 0.7 sum_3.1.earlier
  41.9 0.0 copy-start.5
  41.9 2.1 %collective-permute-start.6 = (bf16[512,512]{1,0:T(8,128)(2,1)S(1)}, bf16[512,512]{1,0:T(8,128)(2,1)S(1)}, u32[]{:S(2)}, u32[]{:S(2)}) collective-permute-start(bf16[512,512]{1,0:T(8,128)(2,1)S(1)} %sum_3.1.earlier), channel_id=1, source_target_pairs={{0,28},{1,5},{2,30},{3,7},{4,0},{5,9},{6,2},{7,11},{8,4},{9,13},{1... | collective-permute-start | bytes 1572872 | tf_op jit(solution)/shard_map/ppermute | solution.py:203
  43.9 2.0 %collective-permute-start.5 = (bf16[512,512]{1,0:T(8,128)(2,1)S(1)}, bf16[512,512]{1,0:T(8,128)(2,1)S(1)}, u32[]{:S(2)}, u32[]{:S(2)}) collective-permute-start(bf16[512,512]{1,0:T(8,128)(2,1)S(1)} %collective-permute-done.2.earlier.w7), channel_id=1, source_target_pairs={{0,28},{1,5},{2,30},{3,7},{4,0},{5,9},{6,2},{7,11},{8,4},{9,13},{1... | collective-permute-start | bytes 1572872 | tf_op jit(solution)/shard_map/ppermute | solution.py:203
  45.9 7.2 %collective-permute-done.6.got = bf16[512,512]{1,0:T(8,128)(2,1)S(1)} collective-permute-done((bf16[512,512]{1,0:T(8,128)(2,1)S(1)}, bf16[512,512]{1,0:T(8,128)(2,1)S(1)}, u32[]{:S(2)}, u32[]{:S(2)}) %collective-permute-start.6) | collective-permute-done | bytes 524320 | tf_op jit(solution)/shard_map/ppermute | solution.py:203
  53.2 0.1 sum_2.1
  53.3 1.9 %collective-permute-start.8 = (bf16[512,512]{1,0:T(8,128)(2,1)S(1)}, bf16[512,512]{1,0:T(8,128)(2,1)S(1)}, u32[]{:S(2)}, u32[]{:S(2)}) collective-permute-start(bf16[512,512]{1,0:T(8,128)(2,1)S(1)} %sum_2.1), channel_id=1, source_target_pairs={{0,28},{1,5},{2,30},{3,7},{4,0},{5,9},{6,2},{7,11},{8,4},{9,13},{1... | collective-permute-start | bytes 1572872 | tf_op jit(solution)/shard_map/ppermute | solution.py:203
  55.2 3.5 %collective-permute-done.5.w6 = bf16[512,512]{1,0:T(8,128)(2,1)S(1)} collective-permute-done((bf16[512,512]{1,0:T(8,128)(2,1)S(1)}, bf16[512,512]{1,0:T(8,128)(2,1)S(1)}, u32[]{:S(2)}, u32[]{:S(2)}) %collective-permute-start.5) | collective-permute-done | bytes 524320 | tf_op jit(solution)/shard_map/ppermute | solution.py:203
  58.8 1.9 %collective-permute-start.7 = (bf16[512,512]{1,0:T(8,128)(2,1)S(1)}, bf16[512,512]{1,0:T(8,128)(2,1)S(1)}, u32[]{:S(2)}, u32[]{:S(2)}) collective-permute-start(bf16[512,512]{1,0:T(8,128)(2,1)S(1)} %collective-permute-done.5.w6), channel_id=1, source_target_pairs={{0,28},{1,5},{2,30},{3,7},{4,0},{5,9},{6,2},{7,11},{8,4},{9,13},{1... | collective-permute-start | bytes 1572872 | tf_op jit(solution)/shard_map/ppermute | solution.py:203
  60.7 15.8 %all_to_all.10.pieces = bf16[16,16,512]{2,1,0:T(8,128)(2,1)S(1)} all-to-all(bf16[16,16,512]{2,1,0:T(8,128)(2,1)S(1)} %bitcast.20), channel_id=1, replica_groups=mesh['rep'=16,'fsdp'=32] {'rep'}, dimensions={0} | all-to-all | bytes 524288 | tf_op jit(solution)/shard_map/all_to_all | solution.py:213
  76.5 1.3 %choose.1.earlier = bf16[16,16,512]{2,1,0:T(8,128)(2,1)} custom-call(s32[16]{0:T(128)S(1)} %copy-done.7, bf16[16,16,512]{2,1,0:T(8,128)(2,1)S(1)} %all_to_all.10.pieces), custom_call_target="tpu_custom_call" | custom-call | tf_op jit(solution)/shard_map/choose/pallas_call | solution.py:177
  77.8 0.0 collective-permute-done.8.got
  77.8 0.1 sum_1.1
  77.9 0.0 collective-permute-done.7.w5
  78.0 1.3 %pad_maximum_fusion = bf16[3,512,512]{2,1,0:T(8,128)(2,1)} fusion(bf16[1,512,512]{2,1,0:T(8,128)(2,1)S(1)} %bitcast.18, bf16[1,512,512]{2,1,0:T(8,128)(2,1)S(1)} %bitcast.19, bf16[1,512,512]{2,1,0:T(8,128)(2,1)S(1)} %bitcast.10), kind=kLoop, calls=%fused_computation | loop fusion | flops 1572864 | bytes 3145728 | tf_op jit(solution)/shard_map/stack | solution.py:283
  79.3 9.0 %collective-permute-start.10 = (bf16[3,512,512]{2,1,0:T(8,128)(2,1)}, bf16[3,512,512]{2,1,0:T(8,128)(2,1)}, u32[]{:S(2)}, u32[]{:S(2)}) collective-permute-start(bf16[3,512,512]{2,1,0:T(8,128)(2,1)} %pad_maximum_fusion), channel_id=1, source_target_pairs={{0,1},{1,0},{2,3},{3,2},{4,5},{5,4},{6,7},{7,6},{8,9},{9,8},{10,11... | collective-permute-start | bytes 4718600 | tf_op jit(solution)/shard_map/ppermute | solution.py:203
  88.3 1.9 %collective-permute-start.11 = (bf16[512,512]{1,0:T(8,128)(2,1)S(1)}, bf16[512,512]{1,0:T(8,128)(2,1)S(1)}, u32[]{:S(2)}, u32[]{:S(2)}) collective-permute-start(bf16[512,512]{1,0:T(8,128)(2,1)S(1)} %sum_1.1), channel_id=1, source_target_pairs={{0,28},{1,5},{2,30},{3,7},{4,0},{5,9},{6,2},{7,11},{8,4},{9,13},{1... | collective-permute-start | bytes 1572872 | tf_op jit(solution)/shard_map/ppermute | solution.py:203
  90.2 0.7 constant_dynamic-slice_fusion
  90.9 1.9 %collective-permute-start.9 = (bf16[256,512]{1,0:T(8,128)(2,1)}, bf16[256,512]{1,0:T(8,128)(2,1)S(1)}, u32[]{:S(2)}, u32[]{:S(2)}) collective-permute-start(bf16[256,512]{1,0:T(8,128)(2,1)} %constant_dynamic-slice_fusion), channel_id=1, source_target_pairs={{0,28},{1,5},{2,30},{3,7},{4,0},{5,9},{6,2},{7,11},{8,4},{9,13},{1... | collective-permute-start | bytes 786440 | tf_op jit(solution)/shard_map/ppermute | solution.py:203
  92.9 3.5 %all-to-all-start.1 = ((bf16[16,16,512]{2,1,0:T(8,128)(2,1)}), bf16[16,16,512]{2,1,0:T(8,128)(2,1)S(1)}, u32[]{:S(2)}, u32[]{:S(2)}) async-start(bf16[16,16,512]{2,1,0:T(8,128)(2,1)} %choose.1.earlier), calls=%async_computation.1 | async-start | bytes 524288 | tf_op jit(solution)/shard_map/all_to_all | solution.py:213
  96.4 3.0 %collective-permute-done.11 = bf16[512,512]{1,0:T(8,128)(2,1)S(1)} collective-permute-done((bf16[512,512]{1,0:T(8,128)(2,1)S(1)}, bf16[512,512]{1,0:T(8,128)(2,1)S(1)}, u32[]{:S(2)}, u32[]{:S(2)}) %collective-permute-start.11) | collective-permute-done | bytes 524320 | tf_op jit(solution)/shard_map/ppermute | solution.py:203
  99.4 0.6 core_sum.1
  100.0 1.9 %collective-permute-start.12 = (bf16[2,128,512]{2,1,0:T(8,128)(2,1)S(1)}, bf16[2,128,512]{2,1,0:T(8,128)(2,1)S(1)}, u32[]{:S(2)}, u32[]{:S(2)}) collective-permute-start(bf16[2,128,512]{2,1,0:T(8,128)(2,1)S(1)} %get-tuple-element.51), channel_id=1, source_target_pairs={{0,1},{1,0},{2,3},{3,2},{4,5},{5,4},{6,7},{7,6},{8,9},{9,8},{10,11... | collective-permute-start | bytes 786440 | tf_op jit(solution)/shard_map/ppermute | solution.py:203
  102.0 0.5 collective-permute-done.9.h4
  102.5 1.9 %collective-permute-start.13 = (bf16[256,512]{1,0:T(8,128)(2,1)S(1)}, bf16[256,512]{1,0:T(8,128)(2,1)S(1)}, u32[]{:S(2)}, u32[]{:S(2)}) collective-permute-start(bf16[256,512]{1,0:T(8,128)(2,1)S(1)} %collective-permute-done.9.h4), channel_id=1, source_target_pairs={{0,1},{1,0},{2,3},{3,2},{4,5},{5,4},{6,7},{7,6},{8,9},{9,8},{10,11... | collective-permute-start | bytes 786440 | tf_op jit(solution)/shard_map/ppermute | solution.py:203
  104.4 0.6 y_sum.1
  105.0 0.9 collective-permute-done.13.swapped4
  105.9 4.8 %collective-permute-start.14 = (bf16[1,128,512]{2,1,0:T(8,128)(2,1)S(1)}, bf16[1,128,512]{2,1,0:T(8,128)(2,1)S(1)}, u32[]{:S(2)}, u32[]{:S(2)}) collective-permute-start(bf16[1,128,512]{2,1,0:T(8,128)(2,1)S(1)} %get-tuple-element.56), channel_id=1, source_target_pairs={{0,2},{1,3},{2,0},{3,1},{4,6},{5,7},{6,4},{7,5},{8,10},{9,11},{10,... | collective-permute-start | bytes 393224 | tf_op jit(solution)/shard_map/ppermute | solution.py:203
  110.8 0.0 collective-permute-done.10.swapped
  110.8 8.0 %token_grad.1 = (bf16[240,512]{1,0:T(8,128)(2,1)}, bf16[240,4096]{1,0:T(8,128)(2,1)}) custom-call(s32[16]{0:T(128)} %compare_select_fusion.3.place, bf16[240,4096]{1,0:T(8,128)(2,1)} %tok_in.3, bf16[4096]{0:T(1024)(128)(2,1)} %gain_in.3, f32[240,1]{1,0:T(8,128)} %get-tuple-element.34.inverse, bf16[8,240,512]{2,1,0:T(8,128)(2,1)} %get-tuple-element.35.normed.normed_in, ...), custom_call_target="tpu_custom_call" | custom-call | tf_op jit(solution)/shard_map/token_grad/pallas_call | solution.py:177
  118.8 0.7 collective-permute-done.14.got
  119.5 0.0 all-to-all-done.1
  119.5 0.8 update.1
  (25 shorter events, 0.1 us)
Async XLA Ops:
  0.6 21.0 %copy-start.4 = (bf16[1,128,512]{2,1,0:T(8,128)(2,1)S(1)}, bf16[1,128,512]{2,1,0:T(8,128)(2,1)}, u32[]{:S(2)}) copy-start(bf16[1,128,512]{2,1,0:T(8,128)(2,1)} %weight.1) | copy-start | bytes 393220
  0.6 13.6 %collective-permute-start = (bf16[1,128,512]{2,1,0:T(8,128)(2,1)}, bf16[1,128,512]{2,1,0:T(8,128)(2,1)S(1)}, u32[]{:S(2)}, u32[]{:S(2)}) collective-permute-start(bf16[1,128,512]{2,1,0:T(8,128)(2,1)} %weight.1), channel_id=1, source_target_pairs={{0,2},{1,3},{2,0},{3,1},{4,6},{5,7},{6,4},{7,5},{8,10},{9,11},{10,... | collective-permute-start | bytes 393224 | tf_op jit(solution)/shard_map/ppermute | solution.py:203
  9.6 15.6 %copy-start.6 = (s32[16]{0:T(128)S(1)}, s32[16]{0:T(128)}, u32[]{:S(2)}) copy-start(s32[16]{0:T(128)} %compare_select_fusion.3.place) | copy-start | bytes 196
  9.6 18.1 %copy-start.2 = (bf16[240,512]{1,0:T(8,128)(2,1)S(1)}, bf16[240,512]{1,0:T(8,128)(2,1)}, u32[]{:S(2)}) copy-start(bf16[240,512]{1,0:T(8,128)(2,1)} %cot.5) | copy-start | bytes 737284
  14.2 13.4 %collective-permute-start.3 = (bf16[240,2304]{1,0:T(8,128)(2,1)}, bf16[240,2304]{1,0:T(8,128)(2,1)S(1)}, u32[]{:S(2)}, u32[]{:S(2)}) collective-permute-start(bf16[240,2304]{1,0:T(8,128)(2,1)} %get-tuple-element.38), channel_id=1, source_target_pairs={{0,1},{1,0},{2,3},{3,2},{4,5},{5,4},{6,7},{7,6},{8,9},{9,8},{10,11... | collective-permute-start | bytes 3317768 | tf_op jit(solution)/shard_map/ppermute | solution.py:203
  21.7 3.4 %collective-permute-start.1 = (bf16[2,128,512]{2,1,0:T(8,128)(2,1)S(1)}, bf16[2,128,512]{2,1,0:T(8,128)(2,1)S(1)}, u32[]{:S(2)}, u32[]{:S(2)}) collective-permute-start(bf16[2,128,512]{2,1,0:T(8,128)(2,1)S(1)} %pad_maximum_fusion.1), channel_id=1, source_target_pairs={{0,1},{1,0},{2,3},{3,2},{4,5},{5,4},{6,7},{7,6},{8,9},{9,8},{10,11... | collective-permute-start | bytes 786440 | tf_op jit(solution)/shard_map/ppermute | solution.py:203
  25.7 5.4 %copy-start.3 = (bf16[4,128,512]{2,1,0:T(8,128)(2,1)}, bf16[4,128,512]{2,1,0:T(8,128)(2,1)S(1)}, u32[]{:S(2)}) copy-start(bf16[4,128,512]{2,1,0:T(8,128)(2,1)S(1)} %join.1) | copy-start | bytes 1572868
  25.7 12.6 %collective-permute-start.2 = (bf16[512,512]{1,0:T(8,128)(2,1)S(1)}, bf16[512,512]{1,0:T(8,128)(2,1)S(1)}, u32[]{:S(2)}, u32[]{:S(2)}) collective-permute-start(bf16[512,512]{1,0:T(8,128)(2,1)S(1)} %bitcast.11), channel_id=1, source_target_pairs={{0,28},{1,5},{2,30},{3,7},{4,0},{5,9},{6,2},{7,11},{8,4},{9,13},{1... | collective-permute-start | bytes 1572872 | tf_op jit(solution)/shard_map/ppermute | solution.py:203
  27.7 1.5 %copy-start = (bf16[8,240,512]{2,1,0:T(8,128)(2,1)S(1)}, bf16[8,240,512]{2,1,0:T(8,128)(2,1)}, u32[]{:S(2)}) copy-start(bf16[8,240,512]{2,1,0:T(8,128)(2,1)} %get-tuple-element.35.normed.normed_in) | copy-start | bytes 5898244
  31.1 10.1 %collective-permute-start.4 = (bf16[256,512]{1,0:T(8,128)(2,1)S(1)}, bf16[256,512]{1,0:T(8,128)(2,1)S(1)}, u32[]{:S(2)}, u32[]{:S(2)}) collective-permute-start(bf16[256,512]{1,0:T(8,128)(2,1)S(1)} %get-tuple-element.40), channel_id=1, source_target_pairs={{0,28},{1,5},{2,30},{3,7},{4,0},{5,9},{6,2},{7,11},{8,4},{9,13},{1... | collective-permute-start | bytes 786440 | tf_op jit(solution)/shard_map/ppermute | solution.py:203
  38.4 39.6 %copy-start.1 = (bf16[512,512]{1,0:T(8,128)(2,1)}, bf16[512,512]{1,0:T(8,128)(2,1)S(1)}, u32[]{:S(2)}) copy-start(bf16[512,512]{1,0:T(8,128)(2,1)S(1)} %collective-permute-done.2.earlier.w7) | copy-start | bytes 1572868
  41.9 18.8 %copy-start.5 = (bf16[1,128,512]{2,1,0:T(8,128)(2,1)S(1)}, bf16[1,128,512]{2,1,0:T(8,128)(2,1)}, u32[]{:S(2)}) copy-start(bf16[1,128,512]{2,1,0:T(8,128)(2,1)} %momentum.1) | copy-start | bytes 393220
  41.9 11.3 %collective-permute-start.6 = (bf16[512,512]{1,0:T(8,128)(2,1)S(1)}, bf16[512,512]{1,0:T(8,128)(2,1)S(1)}, u32[]{:S(2)}, u32[]{:S(2)}) collective-permute-start(bf16[512,512]{1,0:T(8,128)(2,1)S(1)} %sum_3.1.earlier), channel_id=1, source_target_pairs={{0,28},{1,5},{2,30},{3,7},{4,0},{5,9},{6,2},{7,11},{8,4},{9,13},{1... | collective-permute-start | bytes 1572872 | tf_op jit(solution)/shard_map/ppermute | solution.py:203
  43.9 14.8 %collective-permute-start.5 = (bf16[512,512]{1,0:T(8,128)(2,1)S(1)}, bf16[512,512]{1,0:T(8,128)(2,1)S(1)}, u32[]{:S(2)}, u32[]{:S(2)}) collective-permute-start(bf16[512,512]{1,0:T(8,128)(2,1)S(1)} %collective-permute-done.2.earlier.w7), channel_id=1, source_target_pairs={{0,28},{1,5},{2,30},{3,7},{4,0},{5,9},{6,2},{7,11},{8,4},{9,13},{1... | collective-permute-start | bytes 1572872 | tf_op jit(solution)/shard_map/ppermute | solution.py:203
  53.2 23.4 %copy-start.7 = (s32[16]{0:T(128)S(1)}, s32[16]{0:T(128)}, u32[]{:S(2)}) copy-start(s32[16]{0:T(128)} %matching.1) | copy-start | bytes 196
  53.3 24.5 %collective-permute-start.8 = (bf16[512,512]{1,0:T(8,128)(2,1)S(1)}, bf16[512,512]{1,0:T(8,128)(2,1)S(1)}, u32[]{:S(2)}, u32[]{:S(2)}) collective-permute-start(bf16[512,512]{1,0:T(8,128)(2,1)S(1)} %sum_2.1), channel_id=1, source_target_pairs={{0,28},{1,5},{2,30},{3,7},{4,0},{5,9},{6,2},{7,11},{8,4},{9,13},{1... | collective-permute-start | bytes 1572872 | tf_op jit(solution)/shard_map/ppermute | solution.py:203
  58.8 19.2 %copy-start.9 = (bf16[512,512]{1,0:T(8,128)(2,1)}, bf16[512,512]{1,0:T(8,128)(2,1)S(1)}, u32[]{:S(2)}) copy-start(bf16[512,512]{1,0:T(8,128)(2,1)S(1)} %collective-permute-done.5.w6) | copy-start | bytes 1572868
  58.8 19.2 %collective-permute-start.7 = (bf16[512,512]{1,0:T(8,128)(2,1)S(1)}, bf16[512,512]{1,0:T(8,128)(2,1)S(1)}, u32[]{:S(2)}, u32[]{:S(2)}) collective-permute-start(bf16[512,512]{1,0:T(8,128)(2,1)S(1)} %collective-permute-done.5.w6), channel_id=1, source_target_pairs={{0,28},{1,5},{2,30},{3,7},{4,0},{5,9},{6,2},{7,11},{8,4},{9,13},{1... | collective-permute-start | bytes 1572872 | tf_op jit(solution)/shard_map/ppermute | solution.py:203
  77.9 12.3 %copy-start.8 = (bf16[512,512]{1,0:T(8,128)(2,1)}, bf16[512,512]{1,0:T(8,128)(2,1)S(1)}, u32[]{:S(2)}) copy-start(bf16[512,512]{1,0:T(8,128)(2,1)S(1)} %collective-permute-done.7.w5) | copy-start | bytes 1572868
  79.3 31.5 %collective-permute-start.10 = (bf16[3,512,512]{2,1,0:T(8,128)(2,1)}, bf16[3,512,512]{2,1,0:T(8,128)(2,1)}, u32[]{:S(2)}, u32[]{:S(2)}) collective-permute-start(bf16[3,512,512]{2,1,0:T(8,128)(2,1)} %pad_maximum_fusion), channel_id=1, source_target_pairs={{0,1},{1,0},{2,3},{3,2},{4,5},{5,4},{6,7},{7,6},{8,9},{9,8},{10,11... | collective-permute-start | bytes 4718600 | tf_op jit(solution)/shard_map/ppermute | solution.py:203
  88.3 11.1 %collective-permute-start.11 = (bf16[512,512]{1,0:T(8,128)(2,1)S(1)}, bf16[512,512]{1,0:T(8,128)(2,1)S(1)}, u32[]{:S(2)}, u32[]{:S(2)}) collective-permute-start(bf16[512,512]{1,0:T(8,128)(2,1)S(1)} %sum_1.1), channel_id=1, source_target_pairs={{0,28},{1,5},{2,30},{3,7},{4,0},{5,9},{6,2},{7,11},{8,4},{9,13},{1... | collective-permute-start | bytes 1572872 | tf_op jit(solution)/shard_map/ppermute | solution.py:203
  90.9 11.6 %collective-permute-start.9 = (bf16[256,512]{1,0:T(8,128)(2,1)}, bf16[256,512]{1,0:T(8,128)(2,1)S(1)}, u32[]{:S(2)}, u32[]{:S(2)}) collective-permute-start(bf16[256,512]{1,0:T(8,128)(2,1)} %constant_dynamic-slice_fusion), channel_id=1, source_target_pairs={{0,28},{1,5},{2,30},{3,7},{4,0},{5,9},{6,2},{7,11},{8,4},{9,13},{1... | collective-permute-start | bytes 786440 | tf_op jit(solution)/shard_map/ppermute | solution.py:203
  92.9 26.6 %all-to-all-start.1 = ((bf16[16,16,512]{2,1,0:T(8,128)(2,1)}), bf16[16,16,512]{2,1,0:T(8,128)(2,1)S(1)}, u32[]{:S(2)}, u32[]{:S(2)}) async-start(bf16[16,16,512]{2,1,0:T(8,128)(2,1)} %choose.1.earlier), calls=%async_computation.1 | async-start | bytes 524288 | tf_op jit(solution)/shard_map/all_to_all | solution.py:213
  100.0 4.4 %collective-permute-start.12 = (bf16[2,128,512]{2,1,0:T(8,128)(2,1)S(1)}, bf16[2,128,512]{2,1,0:T(8,128)(2,1)S(1)}, u32[]{:S(2)}, u32[]{:S(2)}) collective-permute-start(bf16[2,128,512]{2,1,0:T(8,128)(2,1)S(1)} %get-tuple-element.51), channel_id=1, source_target_pairs={{0,1},{1,0},{2,3},{3,2},{4,5},{5,4},{6,7},{7,6},{8,9},{9,8},{10,11... | collective-permute-start | bytes 786440 | tf_op jit(solution)/shard_map/ppermute | solution.py:203
  102.5 8.3 %copy-start.10 = (bf16[256,512]{1,0:T(8,128)(2,1)}, bf16[256,512]{1,0:T(8,128)(2,1)S(1)}, u32[]{:S(2)}) copy-start(bf16[256,512]{1,0:T(8,128)(2,1)S(1)} %collective-permute-done.9.h4) | copy-start | bytes 786436
  102.5 3.4 %collective-permute-start.13 = (bf16[256,512]{1,0:T(8,128)(2,1)S(1)}, bf16[256,512]{1,0:T(8,128)(2,1)S(1)}, u32[]{:S(2)}, u32[]{:S(2)}) collective-permute-start(bf16[256,512]{1,0:T(8,128)(2,1)S(1)} %collective-permute-done.9.h4), channel_id=1, source_target_pairs={{0,1},{1,0},{2,3},{3,2},{4,5},{5,4},{6,7},{7,6},{8,9},{9,8},{10,11... | collective-permute-start | bytes 786440 | tf_op jit(solution)/shard_map/ppermute | solution.py:203
  105.9 4.9 %copy-start.11 = (bf16[256,512]{1,0:T(8,128)(2,1)}, bf16[256,512]{1,0:T(8,128)(2,1)S(1)}, u32[]{:S(2)}) copy-start(bf16[256,512]{1,0:T(8,128)(2,1)S(1)} %collective-permute-done.13.swapped4) | copy-start | bytes 786436
  105.9 13.6 %collective-permute-start.14 = (bf16[1,128,512]{2,1,0:T(8,128)(2,1)S(1)}, bf16[1,128,512]{2,1,0:T(8,128)(2,1)S(1)}, u32[]{:S(2)}, u32[]{:S(2)}) collective-permute-start(bf16[1,128,512]{2,1,0:T(8,128)(2,1)S(1)} %get-tuple-element.56), channel_id=1, source_target_pairs={{0,2},{1,3},{2,0},{3,1},{4,6},{5,7},{6,4},{7,5},{8,10},{9,11},{10,... | collective-permute-start | bytes 393224 | tf_op jit(solution)/shard_map/ppermute | solution.py:203
